TPU v7x, 128 devices: a whole 4x4x4 slice. The times are simulated.
128 devices in a mesh: region: 16 (over x, z), sub: 8 (over y, core).
Axes of the slice: x: 4, y: 4, z: 4, core: 2. Of those that a mesh axis runs over, the one named last changes fastest.
Arguments:
- state: bfloat16 [524288, 256], P(('region', 'sub')), may hold values from -0.94921875 to 0.94921875
- grad_out: float32 [524288, 256], P(('region', 'sub')), may hold values from -8 to 8
- weight: bfloat16 [256, 256], replicated, may hold values from -0.375 to 0.375
- tiles: bfloat16 [24576, 128, 128], P(('region', 'sub')), may hold values from -0.25 to 0.25
- tile_row: int32 [24576], P(('region', 'sub')), may hold values from 0 to 31
- tile_col: int32 [24576], P(('region', 'sub')), may hold values from 0 to 39
- send_rows: int32 [128, 4, 256], P(('region', 'sub')), may hold values from 0 to 4095
Outputs:
- adjoint: float32 [524288, 256], P(('region', 'sub'))
- residual_norms: float32 [3], replicated
All inputs are finite; a program needn't handle non-finite values.
Results may differ from a plain program's by a relative error of at most 0.009.
Values sent between devices are 32-bit elements; how exact they have to be, the bound alone decides.
No kernel may reach another device: no remote copies, remote signals or barrier semaphores. Data moves between devices by JAX's collectives and lax.ppermute only.
A program may use at most 192 MiB of HBM per device.

v0:
```python
import functools

import jax
import jax.numpy as jnp
from jax import lax
from jax.experimental import pallas as pl
from jax.experimental.pallas import tpu as pltpu
from jax.sharding import PartitionSpec as P

ITERS = 3
B = 128
CHUNK = 512
GROUP = 8
OWN_AT = 256
COUNTS_AT = 512
VMEM_LIMIT = 16 * 1024 * 1024

VMEM = pltpu.VMEM
SMEM = pltpu.SMEM


def vmem_specs(n):
    return [pl.BlockSpec(memory_space=VMEM)] * n


def smem_specs(n):
    return [pl.BlockSpec(memory_space=SMEM)] * n


def kept(x):
    return pltpu.with_memory_space_constraint(x, VMEM)


def mix(adjoint_ref, state_ref, weight_ref, mixed_ref, start):
    rows = pl.ds(start, CHUNK)
    state = state_ref[rows, :].astype(jnp.float32)
    scaled = ((1.0 - state * state) * adjoint_ref[rows, :]).astype(jnp.bfloat16)
    mixed_ref[rows, :] = lax.dot_general(
        scaled, weight_ref[...], (((1,), (1,)), ((), ())), preferred_element_type=jnp.float32
    ).astype(jnp.bfloat16)


def add_tiles(plan_ref, begin, groups, turned_ref, mixed_ref, total_ref, base):
    def group(g, carry):
        parts = []
        for u in range(GROUP):
            entry = plan_ref[begin + g * GROUP + u]
            tile = entry & 255
            row = pl.multiple_of(((entry >> 8) & 255) * B, B)
            col = pl.multiple_of((entry >> 16) * B - base, B)
            parts.append(
                (
                    col,
                    jnp.dot(
                        turned_ref[tile],
                        mixed_ref[pl.ds(row, B), :],
                        preferred_element_type=jnp.float32,
                    ),
                )
            )
        for col, part in parts:
            total_ref[pl.ds(col, B), :] += part
        return carry

    lax.fori_loop(0, groups, group, 0)


def ghosts(plan_ref, slots_ref, turned_ref, mixed_ref, ghost_ref, out_refs, own_blocks):
    ghost_ref[...] = jnp.zeros_like(ghost_ref)
    add_tiles(plan_ref, 0, plan_ref[COUNTS_AT], turned_ref, mixed_ref, ghost_ref, own_blocks * B)
    size = out_refs[0].shape[0]
    for slot, out_ref in enumerate(out_refs):
        at = pl.multiple_of(slots_ref[slot] * size, size)
        out_ref[...] = ghost_ref[pl.ds(at, size), :]


def scatter(adjoint_ref, slots_ref, targets_ref, in_refs):
    size = in_refs[0].shape[0]
    for slot, in_ref in enumerate(in_refs):
        direction = slots_ref[4 + slot]

        def step(g, carry):
            for u in range(8):
                k = g * 8 + u
                row = targets_ref[direction * size + k]
                adjoint_ref[pl.ds(row, 1), :] += in_ref[pl.ds(k, 1), :]
            return carry

        lax.fori_loop(0, size // 8, step, 0)


def first_kernel(
    own_blocks, rows_ref, cols_ref, slots_ref, weight_ref, state_hbm, grad_hbm, tiles_hbm,
    state_ref, grad_ref, turned_ref, mixed_ref, plan_ref, g0, g1, g2, g3,
    tiles_ref, ghost_ref, sems,
):
    tile_count = tiles_hbm.shape[0]
    half = grad_hbm.shape[0] // 2
    loads = []
    for h in range(2):
        at = pl.ds(h * half, half)
        loads.append(pltpu.make_async_copy(state_hbm.at[at], state_ref.at[at], sems.at[2 * h]))
        loads.append(pltpu.make_async_copy(grad_hbm.at[at], grad_ref.at[at], sems.at[2 * h + 1]))
    quarter = tile_count // 4
    for q in range(4):
        at = pl.ds(q * quarter, quarter)
        loads.append(pltpu.make_async_copy(tiles_hbm.at[at], tiles_ref.at[at], sems.at[4 + q]))
    for load in loads:
        load.start()

    def clear(i, carry):
        plan_ref[i] = tile_count + own_blocks * 65536
        plan_ref[OWN_AT + i] = tile_count
        return carry

    lax.fori_loop(0, OWN_AT, clear, 0)

    def place(t, counts):
        ghost_count, own_count = counts
        col = cols_ref[t]
        is_ghost = (col >= own_blocks).astype(jnp.int32)
        at = jnp.where(is_ghost == 1, ghost_count, OWN_AT + own_count)
        plan_ref[at] = t + rows_ref[t] * 256 + col * 65536
        return ghost_count + is_ghost, own_count + 1 - is_ghost

    ghost_count, own_count = lax.fori_loop(0, tile_count, place, (jnp.int32(0), jnp.int32(0)))
    plan_ref[COUNTS_AT] = (ghost_count + GROUP - 1) // GROUP
    plan_ref[COUNTS_AT + 1] = (own_count + GROUP - 1) // GROUP

    for h in range(2):
        loads[2 * h].wait()
        loads[2 * h + 1].wait()

        @pl.loop(0, half // CHUNK)
        def _(i):
            mix(grad_ref, state_ref, weight_ref, mixed_ref,
                pl.multiple_of(h * half + i * CHUNK, CHUNK))

    eye = (
        lax.broadcasted_iota(jnp.int32, (B, B), 0) == lax.broadcasted_iota(jnp.int32, (B, B), 1)
    ).astype(jnp.bfloat16)
    for q in range(4):
        loads[4 + q].wait()

        @pl.loop(0, quarter // 8)
        def _(i):
            for u in range(8):
                t = q * quarter + i * 8 + u
                turned_ref[t] = lax.dot_general(
                    eye, tiles_ref[t], (((1,), (1,)), ((), ())), preferred_element_type=jnp.float32
                ).astype(jnp.bfloat16)

    turned_ref[tile_count] = jnp.zeros((B, B), jnp.bfloat16)
    ghosts(plan_ref, slots_ref, turned_ref, mixed_ref, ghost_ref, (g0, g1, g2, g3), own_blocks)


def own_kernel(measured, plan_ref, turned_ref, mixed_ref, grad_ref, *refs):
    if measured:
        now_ref, before_ref, out_ref, change_ref = refs
        change(now_ref, before_ref, change_ref)
    else:
        (out_ref,) = refs
    out_ref[...] = grad_ref[...]
    add_tiles(
        plan_ref, OWN_AT, plan_ref[COUNTS_AT + 1], turned_ref, mixed_ref, out_ref, 0
    )


def change(now_ref, before_ref, change_ref):
    def step(i, total):
        at = pl.ds(pl.multiple_of(i * 128, 128), 128)
        moved = now_ref[at, :] - before_ref[at, :]
        squares = (moved * moved).reshape(16, 8, 256)
        return total + jnp.sum(squares, axis=0)

    total = lax.fori_loop(
        0, now_ref.shape[0] // 128, step, jnp.zeros((8, 256), jnp.float32)
    )
    change_ref[...] = total[:, :128] + total[:, 128:]


def middle_kernel(
    own_blocks, slots_ref, targets_ref, plan_ref, weight_ref, state_ref, turned_ref, i0, i1, i2, i3, partial_ref,
    adjoint_ref, mixed_ref, g0, g1, g2, g3, ghost_ref,
):
    scatter(adjoint_ref, slots_ref, targets_ref, (i0, i1, i2, i3))

    @pl.loop(0, adjoint_ref.shape[0] // CHUNK)
    def _(i):
        mix(adjoint_ref, state_ref, weight_ref, mixed_ref, pl.multiple_of(i * CHUNK, CHUNK))

    ghosts(plan_ref, slots_ref, turned_ref, mixed_ref, ghost_ref, (g0, g1, g2, g3), own_blocks)


def last_kernel(
    slots_ref, targets_ref, i0, i1, i2, i3, before_ref, change0_ref, change1_ref, partial_ref,
    adjoint_ref, sums_ref, change_ref,
):
    scatter(adjoint_ref, slots_ref, targets_ref, (i0, i1, i2, i3))
    change(adjoint_ref, before_ref, change_ref)
    row = lax.broadcasted_iota(jnp.int32, (8, 128), 0)
    sums = jnp.zeros((8, 128), jnp.float32)
    for i, ref in enumerate((change0_ref, change1_ref, change_ref)):
        sums = jnp.where(row == i, jnp.sum(ref[...]), sums)
    sums_ref[...] = sums


def local(state, grad_out, weight, tiles, tile_row, tile_col, send_rows):
    row_count, feature_count = state.shape
    own_blocks = row_count // B
    region_count = lax.axis_size("region")
    sub_count = lax.axis_size("sub")
    tile_count = tiles.shape[0]
    ghost_count = send_rows.shape[2]
    ghost_rows = send_rows.shape[1] * ghost_count
    f32, bf16, i32 = jnp.float32, jnp.bfloat16, jnp.int32

    region_odd = lax.axis_index("region") % 2
    sub_odd = lax.axis_index("sub") % 2
    slots = jnp.stack(
        [region_odd, 1 - region_odd, 2 + sub_odd, 3 - sub_odd,
         1 - region_odd, region_odd, 3 - sub_odd, 2 + sub_odd]
    ).astype(i32)

    def swap(value, axis, count, odd):
        partner = [(((i + odd) ^ 1) - odd) % count for i in range(count)]
        return lax.ppermute(value, axis, list(enumerate(partner)))

    def exchange(outgoing):
        return (
            swap(outgoing[0], "region", region_count, 0),
            swap(outgoing[1], "region", region_count, 1),
            swap(outgoing[2], "sub", sub_count, 0),
            swap(outgoing[3], "sub", sub_count, 1),
        )

    params = pltpu.CompilerParams(vmem_limit_bytes=VMEM_LIMIT)
    state_k, grad_k, turned, mixed, plan, *outgoing = pl.pallas_call(
        functools.partial(first_kernel, own_blocks),
        in_specs=smem_specs(3) + vmem_specs(1) + [pl.BlockSpec(memory_space=pl.ANY)] * 3,
        out_specs=tuple(vmem_specs(4) + smem_specs(1) + vmem_specs(4)),
        out_shape=(
            VMEM((row_count, feature_count), bf16),
            VMEM((row_count, feature_count), f32),
            VMEM((tile_count + 1, B, B), bf16),
            VMEM((row_count, feature_count), bf16),
            jax.ShapeDtypeStruct((COUNTS_AT + 128,), i32),
        ) + (VMEM((ghost_count, feature_count), f32),) * 4,
        scratch_shapes=[
            VMEM((tile_count, B, B), bf16),
            VMEM((ghost_rows, feature_count), f32),
            pltpu.SemaphoreType.DMA((8,)),
        ],
        compiler_params=params,
        name="first",
    )(tile_row, tile_col, slots, weight, state, grad_out, tiles)
    targets = send_rows.reshape(-1)

    before = None
    adjoint = grad_k
    changes = []
    for step in range(ITERS):
        incoming = exchange(outgoing)
        measured = step > 0
        results = pl.pallas_call(
            functools.partial(own_kernel, measured),
            in_specs=smem_specs(1) + vmem_specs(5 if measured else 3),
            out_specs=tuple(vmem_specs(2 if measured else 1)),
            out_shape=(VMEM((row_count, feature_count), f32),)
            + ((VMEM((8, 128), f32),) if measured else ()),
            compiler_params=params,
            cost_estimate=pl.CostEstimate(flops=10_000_000_000, bytes_accessed=16_000_000, transcendentals=0),
            name="own",
        )(plan, kept(turned), kept(mixed), kept(grad_k), *((kept(adjoint), kept(before)) if measured else ()))
        partial = results[0]
        if measured:
            changes.append(results[1])
        before = adjoint
        incoming = [kept(v) for v in incoming]
        if step < ITERS - 1:
            adjoint, mixed, *outgoing = pl.pallas_call(
                functools.partial(middle_kernel, own_blocks),
                in_specs=smem_specs(3) + vmem_specs(8),
                out_specs=tuple(vmem_specs(6)),
                out_shape=(VMEM((row_count, feature_count), f32), VMEM((row_count, feature_count), bf16))
                + (VMEM((ghost_count, feature_count), f32),) * 4,
                scratch_shapes=[VMEM((ghost_rows, feature_count), f32)],
                input_output_aliases={10: 0},
                compiler_params=params,
                name="middle",
            )(slots, targets, plan, weight, kept(state_k), kept(turned), *incoming, kept(partial))
        else:
            adjoint, sums = pl.pallas_call(
                last_kernel,
                in_specs=smem_specs(2) + vmem_specs(8),
                out_specs=tuple(vmem_specs(2)),
                out_shape=(VMEM((row_count, feature_count), f32), VMEM((8, 128), f32)),
                scratch_shapes=[VMEM((8, 128), f32)],
                input_output_aliases={9: 0},
                compiler_params=params,
                name="last",
            )(slots, targets, *incoming, kept(before), kept(changes[0]), kept(changes[1]), kept(partial))

    def reach(value, axis, count, by):
        return value + lax.ppermute(value, axis, [(i, i ^ by) for i in range(count)])

    for by in (1, 2, 6):
        sums = reach(sums, "sub", sub_count, by)
    for by in (1, 3, 4, 12):
        sums = reach(sums, "region", region_count, by)
    inverse_count = 1.0 / (region_count * sub_count * row_count * feature_count)
    residual_norms = jnp.sqrt(sums[:ITERS, 0] * inverse_count + 1e-06)
    return adjoint, residual_norms


def solution(mesh):
    placed = (
        P(("region", "sub"), None),
        P(("region", "sub"), None),
        P(),
        P(("region", "sub"), None, None),
        P(("region", "sub")),
        P(("region", "sub")),
        P(("region", "sub"), None, None),
    )
    return jax.shard_map(
        local,
        mesh=mesh,
        in_specs=placed,
        out_specs=(P(("region", "sub"), None), P()),
        check_vma=False,
    )
```

profile of v0, /device:TPU:0, one launch (start us, length us, event | category | flops | bytes accessed | tf_op | source)
XLA Modules:
  0.0 119.6 jit_solution(9039821509599839257)
XLA Ops:
  0.6 0.1 stack.23.slots_ref
  0.7 2.8 %copy-done = bf16[192,128,128]{2,1,0:T(8,128)(2,1)S(1)} copy-done((bf16[192,128,128]{2,1,0:T(8,128)(2,1)S(1)}, bf16[192,128,128]{2,1,0:T(8,128)(2,1)}, u32[]{:S(2)}) %copy-start) | copy-done | bytes 6291480
  3.5 2.2 %copy-done.1 = f32[4096,256]{1,0:T(8,128)S(1)} copy-done((f32[4096,256]{1,0:T(8,128)S(1)}, f32[4096,256]{1,0:T(8,128)}, u32[]{:S(2)}) %copy-start.1) | copy-done | bytes 4194328
  5.7 1.6 %copy-done.2 = bf16[4096,256]{1,0:T(8,128)(2,1)S(1)} copy-done((bf16[4096,256]{1,0:T(8,128)(2,1)S(1)}, bf16[4096,256]{1,0:T(8,128)(2,1)}, u32[]{:S(2)}) %copy-start.2) | copy-done | bytes 2097176
  7.3 0.9 copy-done.3
  8.2 0.7 copy-done.5
  8.9 0.7 copy-done.6
  9.6 16.9 %first.1 = (bf16[4096,256]{1,0:T(8,128)(2,1)S(1)}, f32[4096,256]{1,0:T(8,128)S(1)}, bf16[193,128,128]{2,1,0:T(8,128)(2,1)S(1)}, bf16[4096,256]{1,0:T(8,128)(2,1)...) custom-call(s32[192]{0:T(256)S(1)} %copy-done.5, ...), custom_call_target="tpu_custom_call" | custom-call | tf_op jit(solution)/shard_map/first/pallas_call | solution.py:238
  26.5 2.7 %collective-permute-start = (f32[256,256]{1,0:T(8,128)S(1)}, f32[256,256]{1,0:T(8,128)S(1)}, u32[]{:S(2)}, u32[]{:S(2)}) collective-permute-start(f32[256,256]{1,0:T(8,128)S(1)} %get-tuple-element.32), channel_id=1, source_target_pairs={{0,8},{8,0},{16,24},{24,16},{32,40},{40,32},{48,56},{56,48},{64,72... | collective-permute-start | bytes 786440 | tf_op jit(solution)/shard_map/ppermute | solution.py:227
  29.2 4.1 %collective-permute-start.1 = (f32[256,256]{1,0:T(8,128)S(1)}, f32[256,256]{1,0:T(8,128)S(1)}, u32[]{:S(2)}, u32[]{:S(2)}) collective-permute-start(f32[256,256]{1,0:T(8,128)S(1)} %get-tuple-element.33), channel_id=1, source_target_pairs={{0,120},{8,16},{16,8},{24,32},{32,24},{40,48},{48,40},{56,64},{64,... | collective-permute-start | bytes 786440 | tf_op jit(solution)/shard_map/ppermute | solution.py:227
  33.3 0.0 collective-permute-start.2
  33.3 3.4 %collective-permute-start.3 = (f32[256,256]{1,0:T(8,128)S(1)}, f32[256,256]{1,0:T(8,128)S(1)}, u32[]{:S(2)}, u32[]{:S(2)}) collective-permute-start(f32[256,256]{1,0:T(8,128)S(1)} %get-tuple-element.35), channel_id=1, source_target_pairs={{0,7},{1,2},{2,1},{3,4},{4,3},{5,6},{6,5},{7,0},{8,15},{9,10},{10,... | collective-permute-start | bytes 786440 | tf_op jit(solution)/shard_map/ppermute | solution.py:227
  36.8 7.1 %own.3.partial_ref = f32[4096,256]{1,0:T(8,128)S(1)} custom-call(s32[640]{0:T(1024)S(1)} %get-tuple-element.29.plan_ref, bf16[193,128,128]{2,1,0:T(8,128)(2,1)S(1)} %get-tuple-element.31.turned_ref, bf16[4096,256]{1,0:T(8,128)(2,1)S(1)} %get-tuple-element.36.mixed_ref, f32[4096,256]{1,0:T(8,128)S(1)} %get-tuple-element.37.grad_ref.refs_1_), custom_call_target="tpu_custom_call" | custom-call | flops 10000000000 | bytes 16000000 | tf_op jit(solution)/shard_map/own/pallas_call | solution.py:265
  43.9 0.0 collective-permute-done.i0
  43.9 0.0 collective-permute-done.1.i1
  43.9 0.0 collective-permute-done.2.i2
  43.9 0.0 collective-permute-done.3.i3
  44.0 8.9 %middle.2 = (f32[4096,256]{1,0:T(8,128)S(1)}, bf16[4096,256]{1,0:T(8,128)(2,1)S(1)}, f32[256,256]{1,0:T(8,128)S(1)}, f32[256,256]{1,0:T(8,128)S(1)}, f32[256,256]{1,0:T(8,128)S(1)}, /*index=5*/f32[256,256]{1,0:T(8,128)S(1)}) custom-call(s32[8]{0:T(128)S(1)} %stack.23.slots_ref, s32[1024]{0:T(1024)S(1)} %bitcast.6, ...), custom_call_target="tpu_custom_call", output_to_operand_aliasing={{0}: (10, {})} | custom-call | tf_op jit(solution)/shard_map/middle/pallas_call | solution.py:281
  52.9 0.1 collective-permute-start.4
  53.0 1.9 %collective-permute-start.5 = (f32[256,256]{1,0:T(8,128)S(1)}, f32[256,256]{1,0:T(8,128)S(1)}, u32[]{:S(2)}, u32[]{:S(2)}) collective-permute-start(f32[256,256]{1,0:T(8,128)S(1)} %get-tuple-element.39), channel_id=1, source_target_pairs={{0,120},{8,16},{16,8},{24,32},{32,24},{40,48},{48,40},{56,64},{64,... | collective-permute-start | bytes 786440 | tf_op jit(solution)/shard_map/ppermute | solution.py:227
  54.9 0.0 collective-permute-start.6
  54.9 2.6 %collective-permute-start.7 = (f32[256,256]{1,0:T(8,128)S(1)}, f32[256,256]{1,0:T(8,128)S(1)}, u32[]{:S(2)}, u32[]{:S(2)}) collective-permute-start(f32[256,256]{1,0:T(8,128)S(1)} %get-tuple-element.41), channel_id=1, source_target_pairs={{0,7},{1,2},{2,1},{3,4},{4,3},{5,6},{6,5},{7,0},{8,15},{9,10},{10,... | collective-permute-start | bytes 786440 | tf_op jit(solution)/shard_map/ppermute | solution.py:227
  57.6 7.9 %own.4 = (f32[4096,256]{1,0:T(8,128)S(1)}, f32[8,128]{1,0:T(8,128)S(1)}) custom-call(s32[640]{0:T(1024)S(1)} %get-tuple-element.29.plan_ref, bf16[193,128,128]{2,1,0:T(8,128)(2,1)S(1)} %get-tuple-element.31.turned_ref, bf16[4096,256]{1,0:T(8,128)(2,1)S(1)} %get-tuple-element.42.mixed_ref, f32[4096,256]{1,0:T(8,128)S(1)} %get-tuple-element.37.grad_ref.refs_1_, ...), custom_call_target="tpu_custom_call" | custom-call | flops 10000000000 | bytes 16000000 | tf_op jit(solution)/shard_map/own/pallas_call | solution.py:265
  65.4 0.0 collective-permute-done.4.i0
  65.5 0.0 collective-permute-done.5.i1
  65.5 0.0 collective-permute-done.6.i2
  65.5 0.0 collective-permute-done.7.i3
  65.5 9.0 %middle.3 = (f32[4096,256]{1,0:T(8,128)S(1)}, bf16[4096,256]{1,0:T(8,128)(2,1)S(1)}, f32[256,256]{1,0:T(8,128)S(1)}, f32[256,256]{1,0:T(8,128)S(1)}, f32[256,256]{1,0:T(8,128)S(1)}, /*index=5*/f32[256,256]{1,0:T(8,128)S(1)}) custom-call(s32[8]{0:T(128)S(1)} %stack.23.slots_ref, s32[1024]{0:T(1024)S(1)} %bitcast.7, ...), custom_call_target="tpu_custom_call", output_to_operand_aliasing={{0}: (10, {})} | custom-call | tf_op jit(solution)/shard_map/middle/pallas_call | solution.py:281
  74.5 0.1 collective-permute-start.8
  74.6 2.4 %collective-permute-start.9 = (f32[256,256]{1,0:T(8,128)S(1)}, f32[256,256]{1,0:T(8,128)S(1)}, u32[]{:S(2)}, u32[]{:S(2)}) collective-permute-start(f32[256,256]{1,0:T(8,128)S(1)} %get-tuple-element.46), channel_id=1, source_target_pairs={{0,120},{8,16},{16,8},{24,32},{32,24},{40,48},{48,40},{56,64},{64,... | collective-permute-start | bytes 786440 | tf_op jit(solution)/shard_map/ppermute | solution.py:227
  77.0 0.9 collective-permute-start.11
  77.9 8.0 %own.5 = (f32[4096,256]{1,0:T(8,128)S(1)}, f32[8,128]{1,0:T(8,128)S(1)}) custom-call(s32[640]{0:T(1024)S(1)} %get-tuple-element.29.plan_ref, bf16[193,128,128]{2,1,0:T(8,128)(2,1)S(1)} %get-tuple-element.31.turned_ref, bf16[4096,256]{1,0:T(8,128)(2,1)S(1)} %get-tuple-element.51.mixed_ref, f32[4096,256]{1,0:T(8,128)S(1)} %get-tuple-element.37.grad_ref.refs_1_, ...), custom_call_target="tpu_custom_call" | custom-call | flops 10000000000 | bytes 16000000 | tf_op jit(solution)/shard_map/own/pallas_call | solution.py:265
  85.9 0.0 collective-permute-done.10.i2
  86.0 6.5 %last.1 = (f32[4096,256]{1,0:T(8,128)S(1)}, f32[8,128]{1,0:T(8,128)S(1)}) custom-call(s32[8]{0:T(128)S(1)} %stack.23.slots_ref, s32[1024]{0:T(1024)S(1)} %bitcast.8, f32[256,256]{1,0:T(8,128)S(1)} %collective-permute-done.8.i0, f32[256,256]{1,0:T(8,128)S(1)} %collective-permute-done.9.i1, ...), custom_call_target="tpu_custom_call", output_to_operand_aliasing={{0}: (9, {})} | custom-call | tf_op jit(solution)/shard_map/last/pallas_call | solution.py:293
  92.4 0.1 collective-permute-start.12
  92.5 1.2 collective-permute-done.12
  93.7 0.9 collective-permute-start.13
  94.6 2.7 %collective-permute-done.13 = f32[8,128]{1,0:T(8,128)S(1)} collective-permute-done((f32[8,128]{1,0:T(8,128)S(1)}, f32[8,128]{1,0:T(8,128)S(1)}, u32[]{:S(2)}, u32[]{:S(2)}) %collective-permute-start.13) | collective-permute-done | bytes 4128 | tf_op jit(solution)/shard_map/ppermute | solution.py:305
  97.3 1.5 %collective-permute-start.14 = (f32[8,128]{1,0:T(8,128)S(1)}, f32[8,128]{1,0:T(8,128)S(1)}, u32[]{:S(2)}, u32[]{:S(2)}) collective-permute-start(f32[8,128]{1,0:T(8,128)S(1)} %add.40), channel_id=1, source_target_pairs={{0,6},{1,7},{2,4},{3,5},{4,2},{5,3},{6,0},{7,1},{8,14},{9,15},{10,... | collective-permute-start | bytes 12296 | tf_op jit(solution)/shard_map/ppermute | solution.py:305
  98.8 3.4 %collective-permute-done.14 = f32[8,128]{1,0:T(8,128)S(1)} collective-permute-done((f32[8,128]{1,0:T(8,128)S(1)}, f32[8,128]{1,0:T(8,128)S(1)}, u32[]{:S(2)}, u32[]{:S(2)}) %collective-permute-start.14) | collective-permute-done | bytes 4128 | tf_op jit(solution)/shard_map/ppermute | solution.py:305
  102.1 3.6 %collective-permute-done.15 = f32[8,128]{1,0:T(8,128)S(1)} collective-permute-done((f32[8,128]{1,0:T(8,128)S(1)}, f32[8,128]{1,0:T(8,128)S(1)}, u32[]{:S(2)}, u32[]{:S(2)}) %collective-permute-start.15) | collective-permute-done | bytes 4128 | tf_op jit(solution)/shard_map/ppermute | solution.py:305
  105.7 4.8 %collective-permute-done.16 = f32[8,128]{1,0:T(8,128)S(1)} collective-permute-done((f32[8,128]{1,0:T(8,128)S(1)}, f32[8,128]{1,0:T(8,128)S(1)}, u32[]{:S(2)}, u32[]{:S(2)}) %collective-permute-start.16) | collective-permute-done | bytes 4128 | tf_op jit(solution)/shard_map/ppermute | solution.py:305
  110.6 0.3 collective-permute-start.17
  110.9 3.3 %collective-permute-done.17 = f32[8,128]{1,0:T(8,128)S(1)} collective-permute-done((f32[8,128]{1,0:T(8,128)S(1)}, f32[8,128]{1,0:T(8,128)S(1)}, u32[]{:S(2)}, u32[]{:S(2)}) %collective-permute-start.17) | collective-permute-done | bytes 4128 | tf_op jit(solution)/shard_map/ppermute | solution.py:305
  114.2 0.3 collective-permute-start.18
  114.5 2.0 %copy.16 = f32[4096,256]{1,0:T(8,128)} copy(f32[4096,256]{1,0:T(8,128)S(1)} %get-tuple-element.56) | data formatting | bytes 8388608
  116.5 2.5 %collective-permute-done.18 = f32[8,128]{1,0:T(8,128)S(1)} collective-permute-done((f32[8,128]{1,0:T(8,128)S(1)}, f32[8,128]{1,0:T(8,128)S(1)}, u32[]{:S(2)}, u32[]{:S(2)}) %collective-permute-start.18) | collective-permute-done | bytes 4128 | tf_op jit(solution)/shard_map/ppermute | solution.py:305
  119.0 0.6 sqrt_reduce_fusion
  (24 shorter events, 0.1 us)
Async XLA Ops:
  0.7 2.8 %copy-start = (bf16[192,128,128]{2,1,0:T(8,128)(2,1)S(1)}, bf16[192,128,128]{2,1,0:T(8,128)(2,1)}, u32[]{:S(2)}) copy-start(bf16[192,128,128]{2,1,0:T(8,128)(2,1)} %tiles_hbm.1) | copy-start | bytes 18874372
  3.5 2.2 %copy-start.1 = (f32[4096,256]{1,0:T(8,128)S(1)}, f32[4096,256]{1,0:T(8,128)}, u32[]{:S(2)}) copy-start(f32[4096,256]{1,0:T(8,128)} %grad_hbm.1) | copy-start | bytes 12582916
  5.7 1.6 %copy-start.2 = (bf16[4096,256]{1,0:T(8,128)(2,1)S(1)}, bf16[4096,256]{1,0:T(8,128)(2,1)}, u32[]{:S(2)}) copy-start(bf16[4096,256]{1,0:T(8,128)(2,1)} %state_hbm.1) | copy-start | bytes 6291460
  7.3 0.9 copy-start.3
  8.2 0.7 copy-start.5
  8.9 0.7 copy-start.6
  26.5 17.4 %collective-permute-start = (f32[256,256]{1,0:T(8,128)S(1)}, f32[256,256]{1,0:T(8,128)S(1)}, u32[]{:S(2)}, u32[]{:S(2)}) collective-permute-start(f32[256,256]{1,0:T(8,128)S(1)} %get-tuple-element.32), channel_id=1, source_target_pairs={{0,8},{8,0},{16,24},{24,16},{32,40},{40,32},{48,56},{56,48},{64,72... | collective-permute-start | bytes 786440 | tf_op jit(solution)/shard_map/ppermute | solution.py:227
  29.2 14.7 %collective-permute-start.1 = (f32[256,256]{1,0:T(8,128)S(1)}, f32[256,256]{1,0:T(8,128)S(1)}, u32[]{:S(2)}, u32[]{:S(2)}) collective-permute-start(f32[256,256]{1,0:T(8,128)S(1)} %get-tuple-element.33), channel_id=1, source_target_pairs={{0,120},{8,16},{16,8},{24,32},{32,24},{40,48},{48,40},{56,64},{64,... | collective-permute-start | bytes 786440 | tf_op jit(solution)/shard_map/ppermute | solution.py:227
  33.3 10.6 %collective-permute-start.2 = (f32[256,256]{1,0:T(8,128)S(1)}, f32[256,256]{1,0:T(8,128)S(1)}, u32[]{:S(2)}, u32[]{:S(2)}) collective-permute-start(f32[256,256]{1,0:T(8,128)S(1)} %get-tuple-element.34), channel_id=1, source_target_pairs={{0,1},{1,0},{2,3},{3,2},{4,5},{5,4},{6,7},{7,6},{8,9},{9,8},{10,11... | collective-permute-start | bytes 786440 | tf_op jit(solution)/shard_map/ppermute | solution.py:227
  33.3 10.6 %collective-permute-start.3 = (f32[256,256]{1,0:T(8,128)S(1)}, f32[256,256]{1,0:T(8,128)S(1)}, u32[]{:S(2)}, u32[]{:S(2)}) collective-permute-start(f32[256,256]{1,0:T(8,128)S(1)} %get-tuple-element.35), channel_id=1, source_target_pairs={{0,7},{1,2},{2,1},{3,4},{4,3},{5,6},{6,5},{7,0},{8,15},{9,10},{10,... | collective-permute-start | bytes 786440 | tf_op jit(solution)/shard_map/ppermute | solution.py:227
  36.8 7.1 %copy-start.7 = (s32[1,4,256]{2,1,0:T(4,128)S(1)}, s32[1,4,256]{2,1,0:T(4,128)}, u32[]{:S(2)}) copy-start(s32[1,4,256]{2,1,0:T(4,128)} %param.13) | copy-start | bytes 12292
  36.8 7.2 %copy-start.4 = (bf16[256,256]{1,0:T(8,128)(2,1)S(1)}, bf16[256,256]{1,0:T(8,128)(2,1)}, u32[]{:S(2)}) copy-start(bf16[256,256]{1,0:T(8,128)(2,1)} %weight_ref.5) | copy-start | bytes 393220
  52.9 12.5 %collective-permute-start.4 = (f32[256,256]{1,0:T(8,128)S(1)}, f32[256,256]{1,0:T(8,128)S(1)}, u32[]{:S(2)}, u32[]{:S(2)}) collective-permute-start(f32[256,256]{1,0:T(8,128)S(1)} %get-tuple-element.38), channel_id=1, source_target_pairs={{0,8},{8,0},{16,24},{24,16},{32,40},{40,32},{48,56},{56,48},{64,72... | collective-permute-start | bytes 786440 | tf_op jit(solution)/shard_map/ppermute | solution.py:227
  53.0 12.5 %collective-permute-start.5 = (f32[256,256]{1,0:T(8,128)S(1)}, f32[256,256]{1,0:T(8,128)S(1)}, u32[]{:S(2)}, u32[]{:S(2)}) collective-permute-start(f32[256,256]{1,0:T(8,128)S(1)} %get-tuple-element.39), channel_id=1, source_target_pairs={{0,120},{8,16},{16,8},{24,32},{32,24},{40,48},{48,40},{56,64},{64,... | collective-permute-start | bytes 786440 | tf_op jit(solution)/shard_map/ppermute | solution.py:227
  54.9 10.5 %collective-permute-start.6 = (f32[256,256]{1,0:T(8,128)S(1)}, f32[256,256]{1,0:T(8,128)S(1)}, u32[]{:S(2)}, u32[]{:S(2)}) collective-permute-start(f32[256,256]{1,0:T(8,128)S(1)} %get-tuple-element.40), channel_id=1, source_target_pairs={{0,1},{1,0},{2,3},{3,2},{4,5},{5,4},{6,7},{7,6},{8,9},{9,8},{10,11... | collective-permute-start | bytes 786440 | tf_op jit(solution)/shard_map/ppermute | solution.py:227
  54.9 10.5 %collective-permute-start.7 = (f32[256,256]{1,0:T(8,128)S(1)}, f32[256,256]{1,0:T(8,128)S(1)}, u32[]{:S(2)}, u32[]{:S(2)}) collective-permute-start(f32[256,256]{1,0:T(8,128)S(1)} %get-tuple-element.41), channel_id=1, source_target_pairs={{0,7},{1,2},{2,1},{3,4},{4,3},{5,6},{6,5},{7,0},{8,15},{9,10},{10,... | collective-permute-start | bytes 786440 | tf_op jit(solution)/shard_map/ppermute | solution.py:227
  74.5 11.5 %collective-permute-start.8 = (f32[256,256]{1,0:T(8,128)S(1)}, f32[256,256]{1,0:T(8,128)S(1)}, u32[]{:S(2)}, u32[]{:S(2)}) collective-permute-start(f32[256,256]{1,0:T(8,128)S(1)} %get-tuple-element.45), channel_id=1, source_target_pairs={{0,8},{8,0},{16,24},{24,16},{32,40},{40,32},{48,56},{56,48},{64,72... | collective-permute-start | bytes 786440 | tf_op jit(solution)/shard_map/ppermute | solution.py:227
  74.6 11.4 %collective-permute-start.9 = (f32[256,256]{1,0:T(8,128)S(1)}, f32[256,256]{1,0:T(8,128)S(1)}, u32[]{:S(2)}, u32[]{:S(2)}) collective-permute-start(f32[256,256]{1,0:T(8,128)S(1)} %get-tuple-element.46), channel_id=1, source_target_pairs={{0,120},{8,16},{16,8},{24,32},{32,24},{40,48},{48,40},{56,64},{64,... | collective-permute-start | bytes 786440 | tf_op jit(solution)/shard_map/ppermute | solution.py:227
  77.0 9.0 %collective-permute-start.10 = (f32[256,256]{1,0:T(8,128)S(1)}, f32[256,256]{1,0:T(8,128)S(1)}, u32[]{:S(2)}, u32[]{:S(2)}) collective-permute-start(f32[256,256]{1,0:T(8,128)S(1)} %get-tuple-element.47), channel_id=1, source_target_pairs={{0,1},{1,0},{2,3},{3,2},{4,5},{5,4},{6,7},{7,6},{8,9},{9,8},{10,11... | collective-permute-start | bytes 786440 | tf_op jit(solution)/shard_map/ppermute | solution.py:227
  77.0 9.0 %collective-permute-start.11 = (f32[256,256]{1,0:T(8,128)S(1)}, f32[256,256]{1,0:T(8,128)S(1)}, u32[]{:S(2)}, u32[]{:S(2)}) collective-permute-start(f32[256,256]{1,0:T(8,128)S(1)} %get-tuple-element.48), channel_id=1, source_target_pairs={{0,7},{1,2},{2,1},{3,4},{4,3},{5,6},{6,5},{7,0},{8,15},{9,10},{10,... | collective-permute-start | bytes 786440 | tf_op jit(solution)/shard_map/ppermute | solution.py:227
  92.4 1.2 %collective-permute-start.12 = (f32[8,128]{1,0:T(8,128)S(1)}, f32[8,128]{1,0:T(8,128)S(1)}, u32[]{:S(2)}, u32[]{:S(2)}) collective-permute-start(f32[8,128]{1,0:T(8,128)S(1)} %get-tuple-element.55), channel_id=1, source_target_pairs={{0,1},{1,0},{2,3},{3,2},{4,5},{5,4},{6,7},{7,6},{8,9},{9,8},{10,11... | collective-permute-start | bytes 12296 | tf_op jit(solution)/shard_map/ppermute | solution.py:305
  93.7 3.6 %collective-permute-start.13 = (f32[8,128]{1,0:T(8,128)S(1)}, f32[8,128]{1,0:T(8,128)S(1)}, u32[]{:S(2)}, u32[]{:S(2)}) collective-permute-start(f32[8,128]{1,0:T(8,128)S(1)} %add.39), channel_id=1, source_target_pairs={{0,2},{1,3},{2,0},{3,1},{4,6},{5,7},{6,4},{7,5},{8,10},{9,11},{10,... | collective-permute-start | bytes 12296 | tf_op jit(solution)/shard_map/ppermute | solution.py:305
  97.3 4.8 %collective-permute-start.14 = (f32[8,128]{1,0:T(8,128)S(1)}, f32[8,128]{1,0:T(8,128)S(1)}, u32[]{:S(2)}, u32[]{:S(2)}) collective-permute-start(f32[8,128]{1,0:T(8,128)S(1)} %add.40), channel_id=1, source_target_pairs={{0,6},{1,7},{2,4},{3,5},{4,2},{5,3},{6,0},{7,1},{8,14},{9,15},{10,... | collective-permute-start | bytes 12296 | tf_op jit(solution)/shard_map/ppermute | solution.py:305
  102.1 3.6 %collective-permute-start.15 = (f32[8,128]{1,0:T(8,128)S(1)}, f32[8,128]{1,0:T(8,128)S(1)}, u32[]{:S(2)}, u32[]{:S(2)}) collective-permute-start(f32[8,128]{1,0:T(8,128)S(1)} %add.41), channel_id=1, source_target_pairs={{0,8},{8,0},{16,24},{24,16},{32,40},{40,32},{48,56},{56,48},{64,72... | collective-permute-start | bytes 12296 | tf_op jit(solution)/shard_map/ppermute | solution.py:305
  105.7 4.8 %collective-permute-start.16 = (f32[8,128]{1,0:T(8,128)S(1)}, f32[8,128]{1,0:T(8,128)S(1)}, u32[]{:S(2)}, u32[]{:S(2)}) collective-permute-start(f32[8,128]{1,0:T(8,128)S(1)} %add.42), channel_id=1, source_target_pairs={{0,24},{8,16},{16,8},{24,0},{32,56},{40,48},{48,40},{56,32},{64,88... | collective-permute-start | bytes 12296 | tf_op jit(solution)/shard_map/ppermute | solution.py:305
  110.6 3.6 %collective-permute-start.17 = (f32[8,128]{1,0:T(8,128)S(1)}, f32[8,128]{1,0:T(8,128)S(1)}, u32[]{:S(2)}, u32[]{:S(2)}) collective-permute-start(f32[8,128]{1,0:T(8,128)S(1)} %add.43), channel_id=1, source_target_pairs={{0,32},{8,40},{16,48},{24,56},{32,0},{40,8},{48,16},{56,24},{64,96... | collective-permute-start | bytes 12296 | tf_op jit(solution)/shard_map/ppermute | solution.py:305
  114.2 4.8 %collective-permute-start.18 = (f32[8,128]{1,0:T(8,128)S(1)}, f32[8,128]{1,0:T(8,128)S(1)}, u32[]{:S(2)}, u32[]{:S(2)}) collective-permute-start(f32[8,128]{1,0:T(8,128)S(1)} %add.44), channel_id=1, source_target_pairs={{0,96},{8,104},{16,112},{24,120},{32,64},{40,72},{48,80},{56,88},{... | collective-permute-start | bytes 12296 | tf_op jit(solution)/shard_map/ppermute | solution.py:305
where the time goes:
time: 120 us
  Pallas kernels  64.3 us (54%)
  waiting for transfers between devices  21.5 us (18%)
  starting transfers between devices  21.3 us (18%)
  local copies, waits for them, and re-layouts  10.9 us (9%)
    pallas_call x3, Pallas kernels, local(): pl.pallas_call(functools.partial(own_kernel, measured), in_specs=smem_spe...  23 us
    ppermute x7, waiting for transfers between devices, reach(): lax.ppermute(value, axis, [(i, i ^ by) for i in range(count)])  21.5 us
    ppermute x12, starting transfers between devices, swap(): return lax.ppermute(value, axis, list(enumerate(partner)))  18.3 us
    pallas_call x2, Pallas kernels, local(): pl.pallas_call(functools.partial(middle_kernel, own_blocks), in_specs=sme...  17.9 us
    pallas_call x1, Pallas kernels, local(): pl.pallas_call(functools.partial(first_kernel, own_blocks), in_specs=smem...  16.9 us
    unnamed x18, local copies, waits for them, and re-layouts  10.9 us
    pallas_call x1, Pallas kernels, local(): pl.pallas_call(last_kernel, in_specs=smem_specs(2) + vmem_specs(8), out_s...  6.47 us
    ppermute x7, starting transfers between devices, reach(): lax.ppermute(value, axis, [(i, i ^ by) for i in range(count)])  3.03 us
  transfers between devices with their start and end apart: 19, of which 7 were waited for; matrix products, arithmetic and copies ran while one was open for 2% of the time, Pallas kernels for 19%

commit v1 on v0

v1 whole, which is shorter than its diff:
```python
import functools

import jax
import jax.numpy as jnp
from jax import lax
from jax.experimental import pallas as pl
from jax.experimental.pallas import tpu as pltpu
from jax.sharding import PartitionSpec as P

ITERS = 3
B = 128
CHUNK = 1024
GROUP = 16
OWN_AT = 256
COUNTS_AT = 512
VMEM_LIMIT = 16 * 1024 * 1024

VMEM = pltpu.VMEM
SMEM = pltpu.SMEM


def vmem_specs(n):
    return [pl.BlockSpec(memory_space=VMEM)] * n


def smem_specs(n):
    return [pl.BlockSpec(memory_space=SMEM)] * n


def in_hbm(x):
    return pltpu.with_memory_space_constraint(x, pltpu.HBM)


def kept(x):
    return pltpu.with_memory_space_constraint(x, VMEM)


def mix(adjoint, state_ref, weight_ref, mixed_ref, rows):
    state = state_ref[rows, :].astype(jnp.float32)
    scaled = ((1.0 - state * state) * adjoint).astype(jnp.bfloat16)
    mixed_ref[rows, :] = lax.dot_general(
        scaled, weight_ref[...], (((1,), (1,)), ((), ())), preferred_element_type=jnp.float32
    ).astype(jnp.bfloat16)


def chunks(row_count):
    def over(body):
        @pl.loop(0, row_count // CHUNK)
        def _(i):
            body(pl.ds(pl.multiple_of(i * CHUNK, CHUNK), CHUNK))

    return over


def add_tiles(plan_ref, begin, groups, tiles_ref, mixed_ref, total_ref, base):
    def group(g, carry):
        parts = []
        for u in range(GROUP):
            entry = plan_ref[begin + g * GROUP + u]
            tile = entry & 255
            row = pl.multiple_of(((entry >> 8) & 255) * B, B)
            col = pl.multiple_of((entry >> 16) * B - base, B)
            part = lax.dot_general(
                tiles_ref[tile], mixed_ref[pl.ds(row, B), :], (((0,), (0,)), ((), ())),
                preferred_element_type=jnp.float32,
            )
            parts.append((col, part))
        for col, part in parts:
            total_ref[pl.ds(col, B), :] += part
        return carry

    lax.fori_loop(0, groups, group, 0)


def ghosts(plan_ref, slots_ref, tiles_ref, mixed_ref, ghost_ref, out_refs, own_blocks):
    ghost_ref[...] = jnp.zeros_like(ghost_ref)
    add_tiles(plan_ref, 0, plan_ref[COUNTS_AT], tiles_ref, mixed_ref, ghost_ref, own_blocks * B)
    size = out_refs[0].shape[0]
    for slot, out_ref in enumerate(out_refs):
        at = pl.multiple_of(slots_ref[slot] * size, size)
        out_ref[...] = ghost_ref[pl.ds(at, size), :]


def gather_incoming(in_refs, incoming_ref):
    size = in_refs[0].shape[0]
    for slot, in_ref in enumerate(in_refs):
        incoming_ref[slot * size:(slot + 1) * size, :] = in_ref[...].astype(jnp.bfloat16)


def first_kernel(
    own_blocks, slots_ref, rows_hbm, cols_hbm, weight_hbm, state_hbm, grad_hbm, tiles_hbm,
    weight_ref, state_ref, grad_ref, tiles_ref, mixed_ref, plan_ref, g0, g1, g2, g3,
    rows_ref, cols_ref, ghost_ref, sems,
):
    tile_count = tiles_hbm.shape[0]
    row_count = grad_hbm.shape[0]
    copies = [
        pltpu.make_async_copy(rows_hbm, rows_ref, sems.at[0]),
        pltpu.make_async_copy(cols_hbm, cols_ref, sems.at[1]),
        pltpu.make_async_copy(weight_hbm, weight_ref, sems.at[2]),
    ]
    parts = row_count // CHUNK
    for p in range(parts):
        at = pl.ds(p * CHUNK, CHUNK)
        copies.append(pltpu.make_async_copy(state_hbm.at[at], state_ref.at[at], sems.at[3 + 2 * p]))
        copies.append(pltpu.make_async_copy(grad_hbm.at[at], grad_ref.at[at], sems.at[4 + 2 * p]))
    copies.append(
        pltpu.make_async_copy(tiles_hbm, tiles_ref.at[pl.ds(0, tile_count)], sems.at[3 + 2 * parts])
    )
    for copy in copies:
        copy.start()
    tiles_ref[tile_count] = jnp.zeros((B, B), jnp.bfloat16)
    copies[0].wait()
    copies[1].wait()

    def place(g, counts):
        ghost_count, own_count = counts
        for u in range(4):
            t = g * 4 + u
            col = cols_ref[t]
            is_ghost = (col >= own_blocks).astype(jnp.int32)
            at = jnp.where(is_ghost == 1, ghost_count, OWN_AT + own_count)
            plan_ref[at] = t + rows_ref[t] * 256 + col * 65536
            ghost_count = ghost_count + is_ghost
            own_count = own_count + 1 - is_ghost
        return ghost_count, own_count

    ghost_count, own_count = lax.fori_loop(
        0, tile_count // 4, place, (jnp.int32(0), jnp.int32(0))
    )
    for u in range(GROUP):
        plan_ref[ghost_count + u] = tile_count + own_blocks * 65536
        plan_ref[OWN_AT + own_count + u] = tile_count
    plan_ref[COUNTS_AT] = (ghost_count + GROUP - 1) // GROUP
    plan_ref[COUNTS_AT + 1] = (own_count + GROUP - 1) // GROUP

    copies[2].wait()
    for p in range(parts):
        copies[3 + 2 * p].wait()
        copies[4 + 2 * p].wait()
        at = pl.ds(p * CHUNK, CHUNK)
        mix(grad_ref[at, :], state_ref, weight_ref, mixed_ref, at)
    copies[-1].wait()
    ghosts(plan_ref, slots_ref, tiles_ref, mixed_ref, ghost_ref, (g0, g1, g2, g3), own_blocks)


def first_own_kernel(
    plan_ref, slots_ref, targets_ref, tiles_ref, mixed_ref, grad_ref, out_ref, route_ref
):
    size = targets_ref.shape[1]
    row_count = grad_ref.shape[0]
    for slot in range(4):
        target = targets_ref[pl.ds(slots_ref[4 + slot], 1), :]

        @pl.loop(0, row_count // 128)
        def _(i):
            at = pl.multiple_of(i * 128, 128)
            agent = lax.broadcasted_iota(jnp.int32, (128, size), 0) + at
            route_ref[pl.ds(at, 128), slot * size:(slot + 1) * size] = jnp.where(
                agent == target, 1.0, 0.0
            ).astype(jnp.bfloat16)

    out_ref[...] = grad_ref[...]
    add_tiles(plan_ref, OWN_AT, plan_ref[COUNTS_AT + 1], tiles_ref, mixed_ref, out_ref, 0)


def own_kernel(plan_ref, tiles_ref, mixed_ref, grad_ref, now_ref, before_ref, out_ref, change_ref):
    change_ref[...] = jnp.zeros_like(change_ref)
    over = chunks(now_ref.shape[0])

    @over
    def _(rows):
        change_ref[...] += squares(now_ref[rows, :] - before_ref[rows, :])

    out_ref[...] = grad_ref[...]
    add_tiles(plan_ref, OWN_AT, plan_ref[COUNTS_AT + 1], tiles_ref, mixed_ref, out_ref, 0)


def squares(moved):
    total = jnp.sum((moved * moved).reshape(-1, 8, moved.shape[1]), axis=0)
    return total[:, :128] + total[:, 128:]


def middle_kernel(
    own_blocks, slots_ref, plan_ref, weight_ref, state_ref, tiles_ref, route_ref, i0, i1, i2, i3,
    partial_ref, adjoint_ref, mixed_ref, g0, g1, g2, g3, incoming_ref, ghost_ref,
):
    gather_incoming((i0, i1, i2, i3), incoming_ref)
    over = chunks(adjoint_ref.shape[0])

    @over
    def _(rows):
        adjoint = partial_ref[rows, :] + jnp.dot(
            route_ref[rows, :], incoming_ref[...], preferred_element_type=jnp.float32
        )
        adjoint_ref[rows, :] = adjoint
        mix(adjoint, state_ref, weight_ref, mixed_ref, rows)

    ghosts(plan_ref, slots_ref, tiles_ref, mixed_ref, ghost_ref, (g0, g1, g2, g3), own_blocks)


def last_kernel(
    route_ref, i0, i1, i2, i3, before_ref, change0_ref, change1_ref, partial_ref,
    adjoint_ref, sums_ref, incoming_ref, change_ref,
):
    gather_incoming((i0, i1, i2, i3), incoming_ref)
    change_ref[...] = jnp.zeros_like(change_ref)
    over = chunks(adjoint_ref.shape[0])

    @over
    def _(rows):
        adjoint = partial_ref[rows, :] + jnp.dot(
            route_ref[rows, :], incoming_ref[...], preferred_element_type=jnp.float32
        )
        adjoint_ref[rows, :] = adjoint
        change_ref[...] += squares(adjoint - before_ref[rows, :])

    row = lax.broadcasted_iota(jnp.int32, (8, 128), 0)
    sums = jnp.zeros((8, 128), jnp.float32)
    for i, ref in enumerate((change0_ref, change1_ref, change_ref)):
        sums = jnp.where(row == i, jnp.sum(ref[...]), sums)
    sums_ref[...] = sums


def local(state, grad_out, weight, tiles, tile_row, tile_col, send_rows):
    row_count, feature_count = state.shape
    own_blocks = row_count // B
    region_count = lax.axis_size("region")
    sub_count = lax.axis_size("sub")
    tile_count = tiles.shape[0]
    ghost_count = send_rows.shape[2]
    ghost_rows = send_rows.shape[1] * ghost_count
    f32, bf16, i32 = jnp.float32, jnp.bfloat16, jnp.int32

    region_odd = lax.axis_index("region") % 2
    sub_odd = lax.axis_index("sub") % 2
    slots = jnp.stack(
        [region_odd, 1 - region_odd, 2 + sub_odd, 3 - sub_odd,
         1 - region_odd, region_odd, 3 - sub_odd, 2 + sub_odd]
    ).astype(i32)

    def swap(value, axis, count, odd):
        partner = [(((i + odd) ^ 1) - odd) % count for i in range(count)]
        return lax.ppermute(value, axis, list(enumerate(partner)))

    def exchange(outgoing):
        return (
            swap(outgoing[0], "region", region_count, 0),
            swap(outgoing[1], "region", region_count, 1),
            swap(outgoing[2], "sub", sub_count, 0),
            swap(outgoing[3], "sub", sub_count, 1),
        )

    params = pltpu.CompilerParams(vmem_limit_bytes=VMEM_LIMIT)
    beside = pl.CostEstimate(flops=10_000_000_000, bytes_accessed=16_000_000, transcendentals=0)
    parts = row_count // CHUNK
    agents_f32 = VMEM((row_count, feature_count), f32)
    agents_bf16 = VMEM((row_count, feature_count), bf16)
    outgoing_shapes = (VMEM((ghost_count, feature_count), f32),) * 4
    incoming_scratch = VMEM((ghost_rows, feature_count), bf16)
    ghost_scratch = VMEM((ghost_rows, feature_count), f32)

    weight_k, state_k, grad_k, tiles_k, mixed, plan, *outgoing = pl.pallas_call(
        functools.partial(first_kernel, own_blocks),
        in_specs=smem_specs(1) + [pl.BlockSpec(memory_space=pltpu.HBM)] * 6,
        out_specs=tuple(vmem_specs(5) + smem_specs(1) + vmem_specs(4)),
        out_shape=(
            VMEM(weight.shape, bf16),
            agents_bf16,
            agents_f32,
            VMEM((tile_count + 1, B, B), bf16),
            agents_bf16,
            jax.ShapeDtypeStruct((COUNTS_AT + 128,), i32),
        )
        + outgoing_shapes,
        scratch_shapes=[
            SMEM((tile_count,), i32),
            SMEM((tile_count,), i32),
            ghost_scratch,
            pltpu.SemaphoreType.DMA((4 + 2 * parts,)),
        ],
        compiler_params=params,
        name="first",
    )(slots, *[in_hbm(v) for v in (tile_row, tile_col, weight, state, grad_out, tiles)])
    weight_k, state_k, grad_k, tiles_k = [kept(v) for v in (weight_k, state_k, grad_k, tiles_k)]

    before = None
    adjoint = grad_k
    changes = []
    for step in range(ITERS):
        incoming = [kept(v) for v in exchange(outgoing)]
        if step == 0:
            partial, route = pl.pallas_call(
                first_own_kernel,
                in_specs=smem_specs(2) + vmem_specs(4),
                out_specs=tuple(vmem_specs(2)),
                out_shape=(agents_f32, VMEM((row_count, ghost_rows), bf16)),
                compiler_params=params,
                cost_estimate=beside,
                name="first_own",
            )(plan, slots, send_rows.reshape(4, ghost_count), tiles_k, kept(mixed), grad_k)
            route = kept(route)
        else:
            partial, moved = pl.pallas_call(
                own_kernel,
                in_specs=smem_specs(1) + vmem_specs(5),
                out_specs=tuple(vmem_specs(2)),
                out_shape=(agents_f32, VMEM((8, 128), f32)),
                compiler_params=params,
                cost_estimate=beside,
                name="own",
            )(plan, tiles_k, kept(mixed), grad_k, kept(adjoint), kept(before))
            changes.append(kept(moved))
        before = adjoint
        if step < ITERS - 1:
            adjoint, mixed, *outgoing = pl.pallas_call(
                functools.partial(middle_kernel, own_blocks),
                in_specs=smem_specs(2) + vmem_specs(9),
                out_specs=tuple(vmem_specs(6)),
                out_shape=(agents_f32, agents_bf16) + outgoing_shapes,
                scratch_shapes=[incoming_scratch, ghost_scratch],
                input_output_aliases={10: 0},
                compiler_params=params,
                name="middle",
            )(slots, plan, weight_k, state_k, tiles_k, route, *incoming, kept(partial))
        else:
            adjoint, sums = pl.pallas_call(
                last_kernel,
                in_specs=vmem_specs(9),
                out_specs=tuple(vmem_specs(2)),
                out_shape=(agents_f32, VMEM((8, 128), f32)),
                scratch_shapes=[incoming_scratch, VMEM((8, 128), f32)],
                input_output_aliases={8: 0},
                compiler_params=params,
                name="last",
            )(route, *incoming, kept(before), *changes, kept(partial))

    def reach(value, axis, count, by):
        return value + lax.ppermute(value, axis, [(i, i ^ by) for i in range(count)])

    for by in (1, 2, 6):
        sums = reach(sums, "sub", sub_count, by)
    for by in (1, 3, 4, 12):
        sums = reach(sums, "region", region_count, by)
    inverse_count = 1.0 / (region_count * sub_count * row_count * feature_count)
    residual_norms = jnp.sqrt(sums[:ITERS, 0] * inverse_count + 1e-06)
    return adjoint, residual_norms


def solution(mesh):
    placed = (
        P(("region", "sub"), None),
        P(("region", "sub"), None),
        P(),
        P(("region", "sub"), None, None),
        P(("region", "sub")),
        P(("region", "sub")),
        P(("region", "sub"), None, None),
    )
    return jax.shard_map(
        local,
        mesh=mesh,
        in_specs=placed,
        out_specs=(P(("region", "sub"), None), P()),
        check_vma=False,
    )
```

time: 120 us -> 90.6 us (0.76)
  Pallas kernels: 64.3 us -> 43.9 us
  local copies, waits for them, and re-layouts: 10.9 us -> 2.1 us
    pallas_call x1, Pallas kernels: 16.9 us -> 7.53 us  [local(): pl.pallas_call(functools.partial(first_kernel, own_blocks), in_specs=smem...]
    unnamed x18 -> x3, local copies, waits for them, and re-layouts: 10.9 us -> 2.02 us
    pallas_call x4, Pallas kernels: 29.5 us -> 23.8 us  [the longest x2 12.6 us: local(): pl.pallas_call(own_kernel, in_specs=smem_specs(1) + vmem_specs(5), out_sp...]
    pallas_call x2, Pallas kernels: 17.9 us -> 12.5 us  [local(): pl.pallas_call(functools.partial(middle_kernel, own_blocks), in_specs=sme...]
    ppermute x7, starting transfers between devices: 3.03 us -> 4.9 us  [reach(): lax.ppermute(value, axis, [(i, i ^ by) for i in range(count)])]
    ppermute x7, waiting for transfers between devices: 21.5 us -> 19.9 us  [reach(): lax.ppermute(value, axis, [(i, i ^ by) for i in range(count)])]
  transfers between devices with their start and end apart: 19 -> 19, of which waited for: 7 -> 8; matrix products, arithmetic and copies ran while one was open for 2% -> 2% of each run, Pallas kernels for 19% -> 23%
where the time goes in v1:
time: 90.6 us
  Pallas kernels  43.9 us (48%)
  starting transfers between devices  22.1 us (24%)
  waiting for transfers between devices  21 us (23%)
  local copies, waits for them, and re-layouts  2.1 us (2%)
    ppermute x7, waiting for transfers between devices, reach(): lax.ppermute(value, axis, [(i, i ^ by) for i in range(count)])  19.9 us
    ppermute x12, starting transfers between devices, swap(): return lax.ppermute(value, axis, list(enumerate(partner)))  17.2 us
    pallas_call x2, Pallas kernels, local(): pl.pallas_call(own_kernel, in_specs=smem_specs(1) + vmem_specs(5), out_sp...  12.6 us
    pallas_call x2, Pallas kernels, local(): pl.pallas_call(functools.partial(middle_kernel, own_blocks), in_specs=sme...  12.5 us
    pallas_call x1, Pallas kernels, local(): pl.pallas_call(first_own_kernel, in_specs=smem_specs(2) + vmem_specs(4),...  7.93 us
    pallas_call x1, Pallas kernels, local(): pl.pallas_call(functools.partial(first_kernel, own_blocks), in_specs=smem...  7.53 us
    ppermute x7, starting transfers between devices, reach(): lax.ppermute(value, axis, [(i, i ^ by) for i in range(count)])  4.9 us
    pallas_call x1, Pallas kernels, local(): pl.pallas_call(last_kernel, in_specs=vmem_specs(9), out_specs=tuple(vmem_...  3.33 us
  transfers between devices with their start and end apart: 19, of which 8 were waited for; matrix products, arithmetic and copies ran while one was open for 2% of the time, Pallas kernels for 23%

profile of v1, /device:TPU:0, one launch (start us, length us, event | category | flops | bytes accessed | tf_op | source)
XLA Modules:
  0.0 90.6 jit_solution(7345704627656198652)
XLA Ops:
  0.6 0.1 stack.23.slots_ref
  0.7 7.5 %first.1 = (bf16[256,256]{1,0:T(8,128)(2,1)S(1)}, bf16[4096,256]{1,0:T(8,128)(2,1)S(1)}, f32[4096,256]{1,0:T(8,128)S(1)}, bf16[193,128,128]{2,1,0:T(8,128)(2,1)S...) custom-call(s32[8]{0:T(128)S(1)} %stack.23.slots_ref, ...), custom_call_target="tpu_custom_call" | custom-call | tf_op jit(solution)/shard_map/first/pallas_call | solution.py:263
  8.3 2.1 %collective-permute-start = (f32[256,256]{1,0:T(8,128)S(1)}, f32[256,256]{1,0:T(8,128)S(1)}, u32[]{:S(2)}, u32[]{:S(2)}) collective-permute-start(f32[256,256]{1,0:T(8,128)S(1)} %get-tuple-element.39), channel_id=1, source_target_pairs={{0,8},{8,0},{16,24},{24,16},{32,40},{40,32},{48,56},{56,48},{64,72... | collective-permute-start | bytes 786440 | tf_op jit(solution)/shard_map/ppermute | solution.py:244
  10.4 4.7 %collective-permute-start.1 = (f32[256,256]{1,0:T(8,128)S(1)}, f32[256,256]{1,0:T(8,128)S(1)}, u32[]{:S(2)}, u32[]{:S(2)}) collective-permute-start(f32[256,256]{1,0:T(8,128)S(1)} %get-tuple-element.40), channel_id=1, source_target_pairs={{0,120},{8,16},{16,8},{24,32},{32,24},{40,48},{48,40},{56,64},{64,... | collective-permute-start | bytes 786440 | tf_op jit(solution)/shard_map/ppermute | solution.py:244
  15.1 0.0 collective-permute-start.2
  15.1 3.1 %collective-permute-start.3 = (f32[256,256]{1,0:T(8,128)S(1)}, f32[256,256]{1,0:T(8,128)S(1)}, u32[]{:S(2)}, u32[]{:S(2)}) collective-permute-start(f32[256,256]{1,0:T(8,128)S(1)} %get-tuple-element.42), channel_id=1, source_target_pairs={{0,7},{1,2},{2,1},{3,4},{4,3},{5,6},{6,5},{7,0},{8,15},{9,10},{10,... | collective-permute-start | bytes 786440 | tf_op jit(solution)/shard_map/ppermute | solution.py:244
  18.2 7.9 %first_own.1 = (f32[4096,256]{1,0:T(8,128)S(1)}, bf16[4096,1024]{1,0:T(8,128)(2,1)S(1)}) custom-call(s32[640]{0:T(1024)S(1)} %get-tuple-element.32.plan_ref, s32[8]{0:T(128)S(1)} %stack.23.slots_ref, s32[4,256]{1,0:T(4,128)S(1)} %bitcast.5, bf16[193,128,128]{2,1,0:T(8,128)(2,1)S(1)} %get-tuple-element.33.tiles_ref, ...), custom_call_target="tpu_custom_call" | custom-call | flops 10000000000 | bytes 16000000 | tf_op jit(solution)/shard_map/first_own/pallas_call | solution.py:293
  26.1 0.0 collective-permute-done.i0
  26.2 0.0 collective-permute-done.1.i1
  26.2 0.0 collective-permute-done.2.i2
  26.2 0.0 collective-permute-done.3.i3
  26.2 6.2 %middle.2 = (f32[4096,256]{1,0:T(8,128)S(1)}, bf16[4096,256]{1,0:T(8,128)(2,1)S(1)}, f32[256,256]{1,0:T(8,128)S(1)}, f32[256,256]{1,0:T(8,128)S(1)}, f32[256,256]{1,0:T(8,128)S(1)}, /*index=5*/f32[256,256]{1,0:T(8,128)S(1)}) custom-call(s32[8]{0:T(128)S(1)} %stack.23.slots_ref, ...), custom_call_target="tpu_custom_call", output_to_operand_aliasing={{0}: (10, {})} | custom-call | tf_op jit(solution)/shard_map/middle/pallas_call | solution.py:316
  32.4 0.1 collective-permute-start.4
  32.5 1.6 %collective-permute-start.5 = (f32[256,256]{1,0:T(8,128)S(1)}, f32[256,256]{1,0:T(8,128)S(1)}, u32[]{:S(2)}, u32[]{:S(2)}) collective-permute-start(f32[256,256]{1,0:T(8,128)S(1)} %get-tuple-element.45), channel_id=1, source_target_pairs={{0,120},{8,16},{16,8},{24,32},{32,24},{40,48},{48,40},{56,64},{64,... | collective-permute-start | bytes 786440 | tf_op jit(solution)/shard_map/ppermute | solution.py:244
  34.2 0.0 collective-permute-start.6
  34.2 1.5 %collective-permute-start.7 = (f32[256,256]{1,0:T(8,128)S(1)}, f32[256,256]{1,0:T(8,128)S(1)}, u32[]{:S(2)}, u32[]{:S(2)}) collective-permute-start(f32[256,256]{1,0:T(8,128)S(1)} %get-tuple-element.47), channel_id=1, source_target_pairs={{0,7},{1,2},{2,1},{3,4},{4,3},{5,6},{6,5},{7,0},{8,15},{9,10},{10,... | collective-permute-start | bytes 786440 | tf_op jit(solution)/shard_map/ppermute | solution.py:244
  35.7 6.3 %own.2 = (f32[4096,256]{1,0:T(8,128)S(1)}, f32[8,128]{1,0:T(8,128)S(1)}) custom-call(s32[640]{0:T(1024)S(1)} %get-tuple-element.32.plan_ref, bf16[193,128,128]{2,1,0:T(8,128)(2,1)S(1)} %get-tuple-element.33.tiles_ref, bf16[4096,256]{1,0:T(8,128)(2,1)S(1)} %get-tuple-element.48.mixed_ref, f32[4096,256]{1,0:T(8,128)S(1)} %get-tuple-element.35.grad_ref.before_ref, ...), custom_call_target="tpu_custom_call" | custom-call | flops 10000000000 | bytes 16000000 | tf_op jit(solution)/shard_map/own/pallas_call | solution.py:304
  42.1 0.0 collective-permute-done.4.i0
  42.1 1.1 %collective-permute-done.5.i1 = f32[256,256]{1,0:T(8,128)S(1)} collective-permute-done((f32[256,256]{1,0:T(8,128)S(1)}, f32[256,256]{1,0:T(8,128)S(1)}, u32[]{:S(2)}, u32[]{:S(2)}) %collective-permute-start.5) | collective-permute-done | bytes 262176 | tf_op jit(solution)/shard_map/ppermute | solution.py:244
  43.2 0.0 collective-permute-done.6.i2
  43.2 0.0 collective-permute-done.7.i3
  43.2 6.3 %middle.3 = (f32[4096,256]{1,0:T(8,128)S(1)}, bf16[4096,256]{1,0:T(8,128)(2,1)S(1)}, f32[256,256]{1,0:T(8,128)S(1)}, f32[256,256]{1,0:T(8,128)S(1)}, f32[256,256]{1,0:T(8,128)S(1)}, /*index=5*/f32[256,256]{1,0:T(8,128)S(1)}) custom-call(s32[8]{0:T(128)S(1)} %stack.23.slots_ref, ...), custom_call_target="tpu_custom_call", output_to_operand_aliasing={{0}: (10, {})} | custom-call | tf_op jit(solution)/shard_map/middle/pallas_call | solution.py:316
  49.5 0.1 collective-permute-start.8
  49.6 2.1 %collective-permute-start.9 = (f32[256,256]{1,0:T(8,128)S(1)}, f32[256,256]{1,0:T(8,128)S(1)}, u32[]{:S(2)}, u32[]{:S(2)}) collective-permute-start(f32[256,256]{1,0:T(8,128)S(1)} %get-tuple-element.52), channel_id=1, source_target_pairs={{0,120},{8,16},{16,8},{24,32},{32,24},{40,48},{48,40},{56,64},{64,... | collective-permute-start | bytes 786440 | tf_op jit(solution)/shard_map/ppermute | solution.py:244
  51.7 0.0 collective-permute-start.10
  51.7 1.8 %collective-permute-start.11 = (f32[256,256]{1,0:T(8,128)S(1)}, f32[256,256]{1,0:T(8,128)S(1)}, u32[]{:S(2)}, u32[]{:S(2)}) collective-permute-start(f32[256,256]{1,0:T(8,128)S(1)} %get-tuple-element.54), channel_id=1, source_target_pairs={{0,7},{1,2},{2,1},{3,4},{4,3},{5,6},{6,5},{7,0},{8,15},{9,10},{10,... | collective-permute-start | bytes 786440 | tf_op jit(solution)/shard_map/ppermute | solution.py:244
  53.5 6.2 %own.3 = (f32[4096,256]{1,0:T(8,128)S(1)}, f32[8,128]{1,0:T(8,128)S(1)}) custom-call(s32[640]{0:T(1024)S(1)} %get-tuple-element.32.plan_ref, bf16[193,128,128]{2,1,0:T(8,128)(2,1)S(1)} %get-tuple-element.33.tiles_ref, bf16[4096,256]{1,0:T(8,128)(2,1)S(1)} %get-tuple-element.57.mixed_ref, f32[4096,256]{1,0:T(8,128)S(1)} %get-tuple-element.35.grad_ref.before_ref, ...), custom_call_target="tpu_custom_call" | custom-call | flops 10000000000 | bytes 16000000 | tf_op jit(solution)/shard_map/own/pallas_call | solution.py:304
  59.7 0.0 collective-permute-done.8.i0
  59.7 0.0 collective-permute-done.9.i1
  59.7 0.0 collective-permute-done.10.i2
  59.8 0.0 collective-permute-done.11.i3
  59.8 3.3 %last.1 = (f32[4096,256]{1,0:T(8,128)S(1)}, f32[8,128]{1,0:T(8,128)S(1)}) custom-call(bf16[4096,1024]{1,0:T(8,128)(2,1)S(1)} %get-tuple-element.36.route_ref, f32[256,256]{1,0:T(8,128)S(1)} %collective-permute-done.8.i0, f32[256,256]{1,0:T(8,128)S(1)} %collective-permute-done.9.i1, ...), custom_call_target="tpu_custom_call", output_to_operand_aliasing={{0}: (8, {})} | custom-call | tf_op jit(solution)/shard_map/last/pallas_call | solution.py:327
  63.1 0.1 collective-permute-start.12
  63.2 1.2 %collective-permute-done.12 = f32[8,128]{1,0:T(8,128)S(1)} collective-permute-done((f32[8,128]{1,0:T(8,128)S(1)}, f32[8,128]{1,0:T(8,128)S(1)}, u32[]{:S(2)}, u32[]{:S(2)}) %collective-permute-start.12) | collective-permute-done | bytes 4128 | tf_op jit(solution)/shard_map/ppermute | solution.py:339
  64.4 2.3 %collective-permute-start.13 = (f32[8,128]{1,0:T(8,128)S(1)}, f32[8,128]{1,0:T(8,128)S(1)}, u32[]{:S(2)}, u32[]{:S(2)}) collective-permute-start(f32[8,128]{1,0:T(8,128)S(1)} %add.39), channel_id=1, source_target_pairs={{0,2},{1,3},{2,0},{3,1},{4,6},{5,7},{6,4},{7,5},{8,10},{9,11},{10,... | collective-permute-start | bytes 12296 | tf_op jit(solution)/shard_map/ppermute | solution.py:339
  66.7 1.6 %collective-permute-done.13 = f32[8,128]{1,0:T(8,128)S(1)} collective-permute-done((f32[8,128]{1,0:T(8,128)S(1)}, f32[8,128]{1,0:T(8,128)S(1)}, u32[]{:S(2)}, u32[]{:S(2)}) %collective-permute-start.13) | collective-permute-done | bytes 4128 | tf_op jit(solution)/shard_map/ppermute | solution.py:339
  68.3 1.9 %collective-permute-start.14 = (f32[8,128]{1,0:T(8,128)S(1)}, f32[8,128]{1,0:T(8,128)S(1)}, u32[]{:S(2)}, u32[]{:S(2)}) collective-permute-start(f32[8,128]{1,0:T(8,128)S(1)} %add.40), channel_id=1, source_target_pairs={{0,6},{1,7},{2,4},{3,5},{4,2},{5,3},{6,0},{7,1},{8,14},{9,15},{10,... | collective-permute-start | bytes 12296 | tf_op jit(solution)/shard_map/ppermute | solution.py:339
  70.1 2.9 %collective-permute-done.14 = f32[8,128]{1,0:T(8,128)S(1)} collective-permute-done((f32[8,128]{1,0:T(8,128)S(1)}, f32[8,128]{1,0:T(8,128)S(1)}, u32[]{:S(2)}, u32[]{:S(2)}) %collective-permute-start.14) | collective-permute-done | bytes 4128 | tf_op jit(solution)/shard_map/ppermute | solution.py:339
  73.1 0.0 collective-permute-start.15
  73.1 3.6 %collective-permute-done.15 = f32[8,128]{1,0:T(8,128)S(1)} collective-permute-done((f32[8,128]{1,0:T(8,128)S(1)}, f32[8,128]{1,0:T(8,128)S(1)}, u32[]{:S(2)}, u32[]{:S(2)}) %collective-permute-start.15) | collective-permute-done | bytes 4128 | tf_op jit(solution)/shard_map/ppermute | solution.py:339
  76.7 0.5 collective-permute-start.16
  77.2 4.4 %collective-permute-done.16 = f32[8,128]{1,0:T(8,128)S(1)} collective-permute-done((f32[8,128]{1,0:T(8,128)S(1)}, f32[8,128]{1,0:T(8,128)S(1)}, u32[]{:S(2)}, u32[]{:S(2)}) %collective-permute-start.16) | collective-permute-done | bytes 4128 | tf_op jit(solution)/shard_map/ppermute | solution.py:339
  81.5 0.0 collective-permute-start.17
  81.5 3.6 %collective-permute-done.17 = f32[8,128]{1,0:T(8,128)S(1)} collective-permute-done((f32[8,128]{1,0:T(8,128)S(1)}, f32[8,128]{1,0:T(8,128)S(1)}, u32[]{:S(2)}, u32[]{:S(2)}) %collective-permute-start.17) | collective-permute-done | bytes 4128 | tf_op jit(solution)/shard_map/ppermute | solution.py:339
  85.1 0.1 collective-permute-start.18
  85.3 2.0 %copy.15 = f32[4096,256]{1,0:T(8,128)} copy(f32[4096,256]{1,0:T(8,128)S(1)} %get-tuple-element.62) | data formatting | bytes 8388608
  87.3 2.7 %collective-permute-done.18 = f32[8,128]{1,0:T(8,128)S(1)} collective-permute-done((f32[8,128]{1,0:T(8,128)S(1)}, f32[8,128]{1,0:T(8,128)S(1)}, u32[]{:S(2)}, u32[]{:S(2)}) %collective-permute-start.18) | collective-permute-done | bytes 4128 | tf_op jit(solution)/shard_map/ppermute | solution.py:339
  90.0 0.6 sqrt_reduce_fusion
  (9 shorter events, 0.0 us)
Async XLA Ops:
  0.7 17.5 %copy-start = (s32[1,4,256]{2,1,0:T(4,128)S(1)}, s32[1,4,256]{2,1,0:T(4,128)}, u32[]{:S(2)}) copy-start(s32[1,4,256]{2,1,0:T(4,128)} %param.13) | copy-start | bytes 12292
  8.3 17.9 %collective-permute-start = (f32[256,256]{1,0:T(8,128)S(1)}, f32[256,256]{1,0:T(8,128)S(1)}, u32[]{:S(2)}, u32[]{:S(2)}) collective-permute-start(f32[256,256]{1,0:T(8,128)S(1)} %get-tuple-element.39), channel_id=1, source_target_pairs={{0,8},{8,0},{16,24},{24,16},{32,40},{40,32},{48,56},{56,48},{64,72... | collective-permute-start | bytes 786440 | tf_op jit(solution)/shard_map/ppermute | solution.py:244
  10.4 15.8 %collective-permute-start.1 = (f32[256,256]{1,0:T(8,128)S(1)}, f32[256,256]{1,0:T(8,128)S(1)}, u32[]{:S(2)}, u32[]{:S(2)}) collective-permute-start(f32[256,256]{1,0:T(8,128)S(1)} %get-tuple-element.40), channel_id=1, source_target_pairs={{0,120},{8,16},{16,8},{24,32},{32,24},{40,48},{48,40},{56,64},{64,... | collective-permute-start | bytes 786440 | tf_op jit(solution)/shard_map/ppermute | solution.py:244
  15.1 11.1 %collective-permute-start.2 = (f32[256,256]{1,0:T(8,128)S(1)}, f32[256,256]{1,0:T(8,128)S(1)}, u32[]{:S(2)}, u32[]{:S(2)}) collective-permute-start(f32[256,256]{1,0:T(8,128)S(1)} %get-tuple-element.41), channel_id=1, source_target_pairs={{0,1},{1,0},{2,3},{3,2},{4,5},{5,4},{6,7},{7,6},{8,9},{9,8},{10,11... | collective-permute-start | bytes 786440 | tf_op jit(solution)/shard_map/ppermute | solution.py:244
  15.1 11.1 %collective-permute-start.3 = (f32[256,256]{1,0:T(8,128)S(1)}, f32[256,256]{1,0:T(8,128)S(1)}, u32[]{:S(2)}, u32[]{:S(2)}) collective-permute-start(f32[256,256]{1,0:T(8,128)S(1)} %get-tuple-element.42), channel_id=1, source_target_pairs={{0,7},{1,2},{2,1},{3,4},{4,3},{5,6},{6,5},{7,0},{8,15},{9,10},{10,... | collective-permute-start | bytes 786440 | tf_op jit(solution)/shard_map/ppermute | solution.py:244
  32.4 9.6 %collective-permute-start.4 = (f32[256,256]{1,0:T(8,128)S(1)}, f32[256,256]{1,0:T(8,128)S(1)}, u32[]{:S(2)}, u32[]{:S(2)}) collective-permute-start(f32[256,256]{1,0:T(8,128)S(1)} %get-tuple-element.44), channel_id=1, source_target_pairs={{0,8},{8,0},{16,24},{24,16},{32,40},{40,32},{48,56},{56,48},{64,72... | collective-permute-start | bytes 786440 | tf_op jit(solution)/shard_map/ppermute | solution.py:244
  32.5 10.6 %collective-permute-start.5 = (f32[256,256]{1,0:T(8,128)S(1)}, f32[256,256]{1,0:T(8,128)S(1)}, u32[]{:S(2)}, u32[]{:S(2)}) collective-permute-start(f32[256,256]{1,0:T(8,128)S(1)} %get-tuple-element.45), channel_id=1, source_target_pairs={{0,120},{8,16},{16,8},{24,32},{32,24},{40,48},{48,40},{56,64},{64,... | collective-permute-start | bytes 786440 | tf_op jit(solution)/shard_map/ppermute | solution.py:244
  34.2 9.0 %collective-permute-start.6 = (f32[256,256]{1,0:T(8,128)S(1)}, f32[256,256]{1,0:T(8,128)S(1)}, u32[]{:S(2)}, u32[]{:S(2)}) collective-permute-start(f32[256,256]{1,0:T(8,128)S(1)} %get-tuple-element.46), channel_id=1, source_target_pairs={{0,1},{1,0},{2,3},{3,2},{4,5},{5,4},{6,7},{7,6},{8,9},{9,8},{10,11... | collective-permute-start | bytes 786440 | tf_op jit(solution)/shard_map/ppermute | solution.py:244
  34.2 9.0 %collective-permute-start.7 = (f32[256,256]{1,0:T(8,128)S(1)}, f32[256,256]{1,0:T(8,128)S(1)}, u32[]{:S(2)}, u32[]{:S(2)}) collective-permute-start(f32[256,256]{1,0:T(8,128)S(1)} %get-tuple-element.47), channel_id=1, source_target_pairs={{0,7},{1,2},{2,1},{3,4},{4,3},{5,6},{6,5},{7,0},{8,15},{9,10},{10,... | collective-permute-start | bytes 786440 | tf_op jit(solution)/shard_map/ppermute | solution.py:244
  49.5 10.3 %collective-permute-start.8 = (f32[256,256]{1,0:T(8,128)S(1)}, f32[256,256]{1,0:T(8,128)S(1)}, u32[]{:S(2)}, u32[]{:S(2)}) collective-permute-start(f32[256,256]{1,0:T(8,128)S(1)} %get-tuple-element.51), channel_id=1, source_target_pairs={{0,8},{8,0},{16,24},{24,16},{32,40},{40,32},{48,56},{56,48},{64,72... | collective-permute-start | bytes 786440 | tf_op jit(solution)/shard_map/ppermute | solution.py:244
  49.6 10.2 %collective-permute-start.9 = (f32[256,256]{1,0:T(8,128)S(1)}, f32[256,256]{1,0:T(8,128)S(1)}, u32[]{:S(2)}, u32[]{:S(2)}) collective-permute-start(f32[256,256]{1,0:T(8,128)S(1)} %get-tuple-element.52), channel_id=1, source_target_pairs={{0,120},{8,16},{16,8},{24,32},{32,24},{40,48},{48,40},{56,64},{64,... | collective-permute-start | bytes 786440 | tf_op jit(solution)/shard_map/ppermute | solution.py:244
  51.7 8.1 %collective-permute-start.10 = (f32[256,256]{1,0:T(8,128)S(1)}, f32[256,256]{1,0:T(8,128)S(1)}, u32[]{:S(2)}, u32[]{:S(2)}) collective-permute-start(f32[256,256]{1,0:T(8,128)S(1)} %get-tuple-element.53), channel_id=1, source_target_pairs={{0,1},{1,0},{2,3},{3,2},{4,5},{5,4},{6,7},{7,6},{8,9},{9,8},{10,11... | collective-permute-start | bytes 786440 | tf_op jit(solution)/shard_map/ppermute | solution.py:244
  51.7 8.1 %collective-permute-start.11 = (f32[256,256]{1,0:T(8,128)S(1)}, f32[256,256]{1,0:T(8,128)S(1)}, u32[]{:S(2)}, u32[]{:S(2)}) collective-permute-start(f32[256,256]{1,0:T(8,128)S(1)} %get-tuple-element.54), channel_id=1, source_target_pairs={{0,7},{1,2},{2,1},{3,4},{4,3},{5,6},{6,5},{7,0},{8,15},{9,10},{10,... | collective-permute-start | bytes 786440 | tf_op jit(solution)/shard_map/ppermute | solution.py:244
  63.1 1.2 %collective-permute-start.12 = (f32[8,128]{1,0:T(8,128)S(1)}, f32[8,128]{1,0:T(8,128)S(1)}, u32[]{:S(2)}, u32[]{:S(2)}) collective-permute-start(f32[8,128]{1,0:T(8,128)S(1)} %get-tuple-element.61), channel_id=1, source_target_pairs={{0,1},{1,0},{2,3},{3,2},{4,5},{5,4},{6,7},{7,6},{8,9},{9,8},{10,11... | collective-permute-start | bytes 12296 | tf_op jit(solution)/shard_map/ppermute | solution.py:339
  64.4 3.9 %collective-permute-start.13 = (f32[8,128]{1,0:T(8,128)S(1)}, f32[8,128]{1,0:T(8,128)S(1)}, u32[]{:S(2)}, u32[]{:S(2)}) collective-permute-start(f32[8,128]{1,0:T(8,128)S(1)} %add.39), channel_id=1, source_target_pairs={{0,2},{1,3},{2,0},{3,1},{4,6},{5,7},{6,4},{7,5},{8,10},{9,11},{10,... | collective-permute-start | bytes 12296 | tf_op jit(solution)/shard_map/ppermute | solution.py:339
  68.3 4.8 %collective-permute-start.14 = (f32[8,128]{1,0:T(8,128)S(1)}, f32[8,128]{1,0:T(8,128)S(1)}, u32[]{:S(2)}, u32[]{:S(2)}) collective-permute-start(f32[8,128]{1,0:T(8,128)S(1)} %add.40), channel_id=1, source_target_pairs={{0,6},{1,7},{2,4},{3,5},{4,2},{5,3},{6,0},{7,1},{8,14},{9,15},{10,... | collective-permute-start | bytes 12296 | tf_op jit(solution)/shard_map/ppermute | solution.py:339
  73.1 3.6 %collective-permute-start.15 = (f32[8,128]{1,0:T(8,128)S(1)}, f32[8,128]{1,0:T(8,128)S(1)}, u32[]{:S(2)}, u32[]{:S(2)}) collective-permute-start(f32[8,128]{1,0:T(8,128)S(1)} %add.41), channel_id=1, source_target_pairs={{0,8},{8,0},{16,24},{24,16},{32,40},{40,32},{48,56},{56,48},{64,72... | collective-permute-start | bytes 12296 | tf_op jit(solution)/shard_map/ppermute | solution.py:339
  76.7 4.8 %collective-permute-start.16 = (f32[8,128]{1,0:T(8,128)S(1)}, f32[8,128]{1,0:T(8,128)S(1)}, u32[]{:S(2)}, u32[]{:S(2)}) collective-permute-start(f32[8,128]{1,0:T(8,128)S(1)} %add.42), channel_id=1, source_target_pairs={{0,24},{8,16},{16,8},{24,0},{32,56},{40,48},{48,40},{56,32},{64,88... | collective-permute-start | bytes 12296 | tf_op jit(solution)/shard_map/ppermute | solution.py:339
  81.5 3.6 %collective-permute-start.17 = (f32[8,128]{1,0:T(8,128)S(1)}, f32[8,128]{1,0:T(8,128)S(1)}, u32[]{:S(2)}, u32[]{:S(2)}) collective-permute-start(f32[8,128]{1,0:T(8,128)S(1)} %add.43), channel_id=1, source_target_pairs={{0,32},{8,40},{16,48},{24,56},{32,0},{40,8},{48,16},{56,24},{64,96... | collective-permute-start | bytes 12296 | tf_op jit(solution)/shard_map/ppermute | solution.py:339
  85.1 4.8 %collective-permute-start.18 = (f32[8,128]{1,0:T(8,128)S(1)}, f32[8,128]{1,0:T(8,128)S(1)}, u32[]{:S(2)}, u32[]{:S(2)}) collective-permute-start(f32[8,128]{1,0:T(8,128)S(1)} %add.44), channel_id=1, source_target_pairs={{0,96},{8,104},{16,112},{24,120},{32,64},{40,72},{48,80},{56,88},{... | collective-permute-start | bytes 12296 | tf_op jit(solution)/shard_map/ppermute | solution.py:339

commit v2 on v1

v2 whole, which is shorter than its diff:
```python
import functools

import jax
import jax.numpy as jnp
from jax import lax
from jax.experimental import pallas as pl
from jax.experimental.pallas import tpu as pltpu
from jax.sharding import PartitionSpec as P

ITERS = 3
B = 128
LOAD = 1024
CHUNK = 2048
OWN_GROUP = 16
GHOST_GROUP = 8
SECOND = 128
OWN_AT = 256
COUNTS_AT = 512
VMEM_LIMIT = 16 * 1024 * 1024

VMEM = pltpu.VMEM
SMEM = pltpu.SMEM


def vmem_specs(n):
    return [pl.BlockSpec(memory_space=VMEM)] * n


def smem_specs(n):
    return [pl.BlockSpec(memory_space=SMEM)] * n


def in_hbm(x):
    return pltpu.with_memory_space_constraint(x, pltpu.HBM)


def kept(x):
    return pltpu.with_memory_space_constraint(x, VMEM)


def mix(adjoint, state_ref, weight_ref, mixed_ref, rows):
    state = state_ref[rows, :].astype(jnp.float32)
    scaled = ((1.0 - state * state) * adjoint).astype(jnp.bfloat16)
    mixed_ref[rows, :] = lax.dot_general(
        scaled, weight_ref[...], (((1,), (1,)), ((), ())), preferred_element_type=jnp.float32
    ).astype(jnp.bfloat16)


def chunks(row_count):
    def over(body):
        @pl.loop(0, row_count // CHUNK)
        def _(i):
            body(pl.ds(pl.multiple_of(i * CHUNK, CHUNK), CHUNK))

    return over


def add_tiles(plan_ref, begin, groups, size, tiles_ref, mixed_ref, total_ref, base):
    def rows_of(entry):
        return mixed_ref[pl.ds(pl.multiple_of(((entry >> 8) & 255) * B, B), B), :]

    def group(g, carry):
        parts = []
        for u in range(size):
            first = plan_ref[begin + g * size + u]
            second = plan_ref[begin + SECOND + g * size + u]
            col = pl.multiple_of((first >> 16) * B - base, B)
            part = lax.dot_general(
                jnp.concatenate([tiles_ref[first & 255], tiles_ref[second & 255]], axis=0),
                jnp.concatenate([rows_of(first), rows_of(second)], axis=0),
                (((0,), (0,)), ((), ())),
                preferred_element_type=jnp.float32,
            )
            parts.append((col, part))
        for col, part in parts:
            total_ref[pl.ds(col, B), :] += part
        return carry

    lax.fori_loop(0, groups, group, 0)


def ghosts(plan_ref, slots_ref, tiles_ref, mixed_ref, ghost_ref, out_refs, own_blocks):
    ghost_ref[...] = jnp.zeros_like(ghost_ref)
    add_tiles(
        plan_ref, 0, plan_ref[COUNTS_AT], GHOST_GROUP, tiles_ref, mixed_ref, ghost_ref, own_blocks * B
    )
    size = out_refs[0].shape[0]
    for slot, out_ref in enumerate(out_refs):
        at = pl.multiple_of(slots_ref[slot] * size, size)
        out_ref[...] = ghost_ref[pl.ds(at, size), :]


def gather_incoming(in_refs, incoming_ref):
    size = in_refs[0].shape[0]
    for slot, in_ref in enumerate(in_refs):
        incoming_ref[slot * size:(slot + 1) * size, :] = in_ref[...].astype(jnp.bfloat16)


def first_kernel(
    own_blocks, slots_ref, rows_hbm, cols_hbm, targets_hbm, weight_hbm, state_hbm, grad_hbm, tiles_hbm,
    weight_ref, state_ref, grad_ref, tiles_ref, mixed_ref, route_ref, plan_ref, g0, g1, g2, g3,
    rows_ref, cols_ref, waiting_ref, targets_ref, ghost_ref, sems,
):
    tile_count = tiles_hbm.shape[0]
    row_count = grad_hbm.shape[0]
    size = targets_hbm.shape[1]
    ghost_blocks = targets_hbm.shape[0] * size // B
    copies = [
        pltpu.make_async_copy(rows_hbm, rows_ref, sems.at[0]),
        pltpu.make_async_copy(cols_hbm, cols_ref, sems.at[1]),
        pltpu.make_async_copy(targets_hbm, targets_ref, sems.at[2]),
        pltpu.make_async_copy(weight_hbm, weight_ref, sems.at[3]),
    ]
    parts = row_count // LOAD
    for p in range(parts):
        at = pl.ds(p * LOAD, LOAD)
        copies.append(pltpu.make_async_copy(state_hbm.at[at], state_ref.at[at], sems.at[4 + 2 * p]))
        copies.append(pltpu.make_async_copy(grad_hbm.at[at], grad_ref.at[at], sems.at[5 + 2 * p]))
    copies.append(
        pltpu.make_async_copy(tiles_hbm, tiles_ref.at[pl.ds(0, tile_count)], sems.at[4 + 2 * parts])
    )
    for copy in copies:
        copy.start()
    tiles_ref[tile_count] = jnp.zeros((B, B), jnp.bfloat16)
    for c in range(own_blocks + ghost_blocks):
        waiting_ref[c] = -1
    for copy in copies[:3]:
        copy.wait()

    steps = tile_count // 3
    band = row_count // steps

    def place(g, counts):
        ghost_count, own_count = counts
        for u in range(3):
            t = g * 3 + u
            col = cols_ref[t]
            entry = t + rows_ref[t] * 256
            other = waiting_ref[col]
            paired = (other >= 0).astype(jnp.int32)
            is_ghost = (col >= own_blocks).astype(jnp.int32)
            at = jnp.where(is_ghost == 1, ghost_count, OWN_AT + own_count)
            plan_ref[at] = entry + col * 65536
            plan_ref[at + SECOND] = other
            waiting_ref[col] = jnp.where(paired == 1, -1, entry)
            ghost_count = ghost_count + is_ghost * paired
            own_count = own_count + (1 - is_ghost) * paired
        rows = pl.ds(pl.multiple_of(g * band, band), band)
        agent = lax.broadcasted_iota(jnp.int32, (band, size), 0) + g * band
        for slot in range(4):
            target = targets_ref[pl.ds(slots_ref[4 + slot], 1), :]
            route_ref[rows, slot * size:(slot + 1) * size] = jnp.where(
                agent == target, 1.0, 0.0
            ).astype(jnp.bfloat16)
        return ghost_count, own_count

    counts = lax.fori_loop(0, steps, place, (jnp.int32(0), jnp.int32(0)))

    def close(begin, blocks, count, group):
        for c in blocks:
            other = waiting_ref[c]
            plan_ref[begin + count] = other + c * 65536
            plan_ref[begin + count + SECOND] = tile_count
            count = count + (other >= 0).astype(jnp.int32)
        for u in range(group):
            plan_ref[begin + count + u] = tile_count + blocks[0] * 65536
            plan_ref[begin + count + u + SECOND] = tile_count
        return (count + group - 1) // group

    all_blocks = list(range(own_blocks + ghost_blocks))
    plan_ref[COUNTS_AT] = close(0, all_blocks[own_blocks:], counts[0], GHOST_GROUP)
    plan_ref[COUNTS_AT + 1] = close(OWN_AT, all_blocks[:own_blocks], counts[1], OWN_GROUP)

    copies[3].wait()
    for p in range(parts):
        copies[4 + 2 * p].wait()
        copies[5 + 2 * p].wait()
        at = pl.ds(p * LOAD, LOAD)
        mix(grad_ref[at, :], state_ref, weight_ref, mixed_ref, at)
    copies[-1].wait()
    ghosts(plan_ref, slots_ref, tiles_ref, mixed_ref, ghost_ref, (g0, g1, g2, g3), own_blocks)


def first_own_kernel(plan_ref, tiles_ref, mixed_ref, grad_ref, out_ref):
    out_ref[...] = grad_ref[...]
    add_tiles(
        plan_ref, OWN_AT, plan_ref[COUNTS_AT + 1], OWN_GROUP, tiles_ref, mixed_ref, out_ref, 0
    )


def own_kernel(plan_ref, tiles_ref, mixed_ref, grad_ref, now_ref, before_ref, out_ref, change_ref):
    change_ref[...] = jnp.zeros_like(change_ref)
    over = chunks(now_ref.shape[0])

    @over
    def _(rows):
        change_ref[...] += squares(now_ref[rows, :] - before_ref[rows, :])

    out_ref[...] = grad_ref[...]
    add_tiles(
        plan_ref, OWN_AT, plan_ref[COUNTS_AT + 1], OWN_GROUP, tiles_ref, mixed_ref, out_ref, 0
    )


def squares(moved):
    total = jnp.sum((moved * moved).reshape(-1, 8, moved.shape[1]), axis=0)
    return total[:, :128] + total[:, 128:]


def middle_kernel(
    own_blocks, slots_ref, plan_ref, weight_ref, state_ref, tiles_ref, route_ref, i0, i1, i2, i3,
    partial_ref, adjoint_ref, mixed_ref, g0, g1, g2, g3, incoming_ref, ghost_ref,
):
    gather_incoming((i0, i1, i2, i3), incoming_ref)
    over = chunks(adjoint_ref.shape[0])

    @over
    def _(rows):
        adjoint = partial_ref[rows, :] + jnp.dot(
            route_ref[rows, :], incoming_ref[...], preferred_element_type=jnp.float32
        )
        adjoint_ref[rows, :] = adjoint
        mix(adjoint, state_ref, weight_ref, mixed_ref, rows)

    ghosts(plan_ref, slots_ref, tiles_ref, mixed_ref, ghost_ref, (g0, g1, g2, g3), own_blocks)


def last_kernel(
    route_ref, i0, i1, i2, i3, before_ref, change0_ref, change1_ref, partial_ref,
    adjoint_hbm, sums_ref, incoming_ref, adjoint_ref, sems,
):
    gather_incoming((i0, i1, i2, i3), incoming_ref)
    row_count = partial_ref.shape[0]
    change = jnp.zeros((8, 128), jnp.float32)
    copies = []
    for p in range(row_count // LOAD):
        rows = pl.ds(p * LOAD, LOAD)
        adjoint = partial_ref[rows, :] + jnp.dot(
            route_ref[rows, :], incoming_ref[...], preferred_element_type=jnp.float32
        )
        adjoint_ref[rows, :] = adjoint
        copies.append(pltpu.make_async_copy(adjoint_ref.at[rows], adjoint_hbm.at[rows], sems.at[p]))
        copies[-1].start()
        change += squares(adjoint - before_ref[rows, :])

    lane = lax.broadcasted_iota(jnp.int32, sums_ref.shape, 1)
    sums = jnp.zeros(sums_ref.shape, jnp.float32)
    for i, value in enumerate((change0_ref[...], change1_ref[...], change)):
        sums = jnp.where(lane == i, jnp.sum(value), sums)
    sums_ref[...] = sums
    for copy in copies:
        copy.wait()


def local(state, grad_out, weight, tiles, tile_row, tile_col, send_rows):
    row_count, feature_count = state.shape
    own_blocks = row_count // B
    region_count = lax.axis_size("region")
    sub_count = lax.axis_size("sub")
    tile_count = tiles.shape[0]
    ghost_count = send_rows.shape[2]
    ghost_rows = send_rows.shape[1] * ghost_count
    f32, bf16, i32 = jnp.float32, jnp.bfloat16, jnp.int32

    region_odd = lax.axis_index("region") % 2
    sub_odd = lax.axis_index("sub") % 2
    slots = jnp.stack(
        [region_odd, 1 - region_odd, 2 + sub_odd, 3 - sub_odd,
         1 - region_odd, region_odd, 3 - sub_odd, 2 + sub_odd]
    ).astype(i32)

    def swap(value, axis, count, odd):
        partner = [(((i + odd) ^ 1) - odd) % count for i in range(count)]
        return lax.ppermute(value, axis, list(enumerate(partner)))

    def exchange(outgoing):
        return (
            swap(outgoing[0], "region", region_count, 0),
            swap(outgoing[1], "region", region_count, 1),
            swap(outgoing[2], "sub", sub_count, 0),
            swap(outgoing[3], "sub", sub_count, 1),
        )

    params = pltpu.CompilerParams(vmem_limit_bytes=VMEM_LIMIT)
    beside = pl.CostEstimate(flops=10_000_000_000, bytes_accessed=16_000_000, transcendentals=0)
    parts = row_count // LOAD
    agents_f32 = VMEM((row_count, feature_count), f32)
    agents_bf16 = VMEM((row_count, feature_count), bf16)
    outgoing_shapes = (VMEM((ghost_count, feature_count), f32),) * 4
    incoming_scratch = VMEM((ghost_rows, feature_count), bf16)
    ghost_scratch = VMEM((ghost_rows, feature_count), f32)

    targets = send_rows.reshape(4, ghost_count)
    weight_k, state_k, grad_k, tiles_k, mixed, route, plan, *outgoing = pl.pallas_call(
        functools.partial(first_kernel, own_blocks),
        in_specs=smem_specs(1) + [pl.BlockSpec(memory_space=pltpu.HBM)] * 7,
        out_specs=tuple(vmem_specs(6) + smem_specs(1) + vmem_specs(4)),
        out_shape=(
            VMEM(weight.shape, bf16),
            agents_bf16,
            agents_f32,
            VMEM((tile_count + 1, B, B), bf16),
            agents_bf16,
            VMEM((row_count, ghost_rows), bf16),
            jax.ShapeDtypeStruct((COUNTS_AT + 128,), i32),
        )
        + outgoing_shapes,
        scratch_shapes=[
            SMEM((tile_count,), i32),
            SMEM((tile_count,), i32),
            SMEM((128,), i32),
            VMEM((4, ghost_count), i32),
            ghost_scratch,
            pltpu.SemaphoreType.DMA((5 + 2 * parts,)),
        ],
        compiler_params=params,
        name="first",
    )(slots, *[in_hbm(v) for v in (tile_row, tile_col, targets, weight, state, grad_out, tiles)])
    weight_k, state_k, grad_k, tiles_k, route = [
        kept(v) for v in (weight_k, state_k, grad_k, tiles_k, route)
    ]

    before = None
    adjoint = grad_k
    changes = []
    for step in range(ITERS):
        incoming = [kept(v) for v in exchange(outgoing)]
        if step == 0:
            (partial,) = pl.pallas_call(
                first_own_kernel,
                in_specs=smem_specs(1) + vmem_specs(3),
                out_specs=tuple(vmem_specs(1)),
                out_shape=(agents_f32,),
                compiler_params=params,
                cost_estimate=beside,
                name="first_own",
            )(plan, tiles_k, kept(mixed), grad_k)
        else:
            partial, moved = pl.pallas_call(
                own_kernel,
                in_specs=smem_specs(1) + vmem_specs(5),
                out_specs=tuple(vmem_specs(2)),
                out_shape=(agents_f32, VMEM((8, 128), f32)),
                compiler_params=params,
                cost_estimate=beside,
                name="own",
            )(plan, tiles_k, kept(mixed), grad_k, kept(adjoint), kept(before))
            changes.append(kept(moved))
        before = adjoint
        if step < ITERS - 1:
            adjoint, mixed, *outgoing = pl.pallas_call(
                functools.partial(middle_kernel, own_blocks),
                in_specs=smem_specs(2) + vmem_specs(9),
                out_specs=tuple(vmem_specs(6)),
                out_shape=(agents_f32, agents_bf16) + outgoing_shapes,
                scratch_shapes=[incoming_scratch, ghost_scratch],
                input_output_aliases={10: 0},
                compiler_params=params,
                name="middle",
            )(slots, plan, weight_k, state_k, tiles_k, route, *incoming, kept(partial))
        else:
            adjoint, sums = pl.pallas_call(
                last_kernel,
                in_specs=vmem_specs(9),
                out_specs=(pl.BlockSpec(memory_space=pltpu.HBM), pl.BlockSpec(memory_space=VMEM)),
                out_shape=(
                    pltpu.HBM((row_count, feature_count), f32),
                    VMEM((region_count * sub_count, 128), f32),
                ),
                scratch_shapes=[incoming_scratch, agents_f32, pltpu.SemaphoreType.DMA((parts,))],
                compiler_params=params,
                name="last",
            )(route, *incoming, kept(before), *changes, kept(partial))

    sums = lax.all_to_all(sums, ("region", "sub"), 0, 0, tiled=True)
    total = jnp.sum(sums, axis=0)
    inverse_count = 1.0 / (region_count * sub_count * row_count * feature_count)
    residual_norms = jnp.sqrt(total[:ITERS] * inverse_count + 1e-06)
    return adjoint, residual_norms


def solution(mesh):
    placed = (
        P(("region", "sub"), None),
        P(("region", "sub"), None),
        P(),
        P(("region", "sub"), None, None),
        P(("region", "sub")),
        P(("region", "sub")),
        P(("region", "sub"), None, None),
    )
    return jax.shard_map(
        local,
        mesh=mesh,
        in_specs=placed,
        out_specs=(P(("region", "sub"), None), P()),
        check_vma=False,
    )
```

time: 90.6 us -> 77.7 us (0.86)
  waiting for transfers between devices: 21 us -> 0.03 us
  blocking collectives: 0 us -> 15.9 us
  Pallas kernels: 43.9 us -> 37.6 us
  local copies, waits for them, and re-layouts: 2.1 us -> 0.09 us
    ppermute x7 -> x0, waiting for transfers between devices: 19.9 us -> none  [reach(): lax.ppermute(value, axis, [(i, i ^ by) for i in range(count)])]
    all_to_all x0 -> x1, blocking collectives: none -> 15.9 us  [local(): sums = lax.all_to_all(sums, ('region', 'sub'), 0, 0, tiled=True)]
    ppermute x7 -> x0, starting transfers between devices: 4.9 us -> none  [reach(): lax.ppermute(value, axis, [(i, i ^ by) for i in range(count)])]
    ppermute x12, starting transfers between devices: 17.2 us -> 22 us  [swap(): return lax.ppermute(value, axis, list(enumerate(partner)))]
    pallas_call x2, Pallas kernels: 11.3 us -> 8.48 us  [the longest x1 4.52 us: local(): pl.pallas_call(first_own_kernel, in_specs=smem_specs(1) + vmem_specs(3),...]
    pallas_call x2, Pallas kernels: 12.6 us -> 9.98 us  [local(): pl.pallas_call(own_kernel, in_specs=smem_specs(1) + vmem_specs(5), out_sp...]
    unnamed x3 -> x0, local copies, waits for them, and re-layouts: 2.02 us -> none
    pallas_call x2, Pallas kernels: 12.5 us -> 10.9 us  [local(): pl.pallas_call(functools.partial(middle_kernel, own_blocks), in_specs=sme...]
  transfers between devices with their start and end apart: 19 -> 12, of which waited for: 8 -> 0; matrix products, arithmetic and copies ran while one was open for 2% -> 0% of each run, Pallas kernels for 23% -> 19%
where the time goes in v2:
time: 77.7 us; the launch traced here: 77.1 us
  Pallas kernels  37.6 us (48%)
  starting transfers between devices  22 us (28%)
  blocking collectives  15.9 us (20%)
  between operations  0.82 us (1%)
    ppermute x12, starting transfers between devices, swap(): return lax.ppermute(value, axis, list(enumerate(partner)))  22 us
    all_to_all x1, blocking collectives, local(): sums = lax.all_to_all(sums, ('region', 'sub'), 0, 0, tiled=True)  15.9 us
    pallas_call x2, Pallas kernels, local(): pl.pallas_call(functools.partial(middle_kernel, own_blocks), in_specs=sme...  10.9 us
    pallas_call x2, Pallas kernels, local(): pl.pallas_call(own_kernel, in_specs=smem_specs(1) + vmem_specs(5), out_sp...  9.98 us
    pallas_call x1, Pallas kernels, local(): pl.pallas_call(functools.partial(first_kernel, own_blocks), in_specs=smem...  8.26 us
    pallas_call x1, Pallas kernels, local(): pl.pallas_call(first_own_kernel, in_specs=smem_specs(1) + vmem_specs(3),...  4.52 us
    pallas_call x1, Pallas kernels, local(): pl.pallas_call(last_kernel, in_specs=vmem_specs(9), out_specs=(pl.BlockSp...  3.96 us
  transfers between devices with their start and end apart: 12, of which 0 were waited for; matrix products, arithmetic and copies ran while one was open for 0% of the time, Pallas kernels for 19%

profile of v2, /device:TPU:0, one launch (start us, length us, event | category | flops | bytes accessed | tf_op | source)
XLA Modules:
  0.0 77.1 jit_solution(9901894391578708806)
XLA Ops:
  0.6 0.1 stack.23.slots_ref
  0.7 8.3 %first.1 = (bf16[256,256]{1,0:T(8,128)(2,1)S(1)}, bf16[4096,256]{1,0:T(8,128)(2,1)S(1)}, f32[4096,256]{1,0:T(8,128)S(1)}, bf16[193,128,128]{2,1,0:T(8,128)(2,1)S...) custom-call(s32[8]{0:T(128)S(1)} %stack.23.slots_ref, ...), custom_call_target="tpu_custom_call" | custom-call | tf_op jit(solution)/shard_map/first/pallas_call | solution.py:294
  9.0 2.1 %collective-permute-start = (f32[256,256]{1,0:T(8,128)S(1)}, f32[256,256]{1,0:T(8,128)S(1)}, u32[]{:S(2)}, u32[]{:S(2)}) collective-permute-start(f32[256,256]{1,0:T(8,128)S(1)} %get-tuple-element.36), channel_id=1, source_target_pairs={{0,8},{8,0},{16,24},{24,16},{32,40},{40,32},{48,56},{56,48},{64,72... | collective-permute-start | bytes 786440 | tf_op jit(solution)/shard_map/ppermute | solution.py:274
  11.1 4.7 %collective-permute-start.1 = (f32[256,256]{1,0:T(8,128)S(1)}, f32[256,256]{1,0:T(8,128)S(1)}, u32[]{:S(2)}, u32[]{:S(2)}) collective-permute-start(f32[256,256]{1,0:T(8,128)S(1)} %get-tuple-element.37), channel_id=1, source_target_pairs={{0,120},{8,16},{16,8},{24,32},{32,24},{40,48},{48,40},{56,64},{64,... | collective-permute-start | bytes 786440 | tf_op jit(solution)/shard_map/ppermute | solution.py:274
  15.8 0.0 collective-permute-start.2
  15.8 3.1 %collective-permute-start.3 = (f32[256,256]{1,0:T(8,128)S(1)}, f32[256,256]{1,0:T(8,128)S(1)}, u32[]{:S(2)}, u32[]{:S(2)}) collective-permute-start(f32[256,256]{1,0:T(8,128)S(1)} %get-tuple-element.39), channel_id=1, source_target_pairs={{0,7},{1,2},{2,1},{3,4},{4,3},{5,6},{6,5},{7,0},{8,15},{9,10},{10,... | collective-permute-start | bytes 786440 | tf_op jit(solution)/shard_map/ppermute | solution.py:274
  18.9 4.5 %first_own.1.partial_ref = f32[4096,256]{1,0:T(8,128)S(1)} custom-call(s32[640]{0:T(1024)S(1)} %get-tuple-element.32.plan_ref, bf16[193,128,128]{2,1,0:T(8,128)(2,1)S(1)} %get-tuple-element.35.tiles_ref, bf16[4096,256]{1,0:T(8,128)(2,1)S(1)} %get-tuple-element.40.mixed_ref, f32[4096,256]{1,0:T(8,128)S(1)} %get-tuple-element.41.grad_ref.before_ref), custom_call_target="tpu_custom_call" | custom-call | flops 10000000000 | bytes 16000000 | tf_op jit(solution)/shard_map/first_own/pallas_call | solution.py:329
  23.5 0.0 collective-permute-done.i0
  23.5 0.0 collective-permute-done.1.i1
  23.5 0.0 collective-permute-done.2.i2
  23.5 0.0 collective-permute-done.3.i3
  23.5 5.5 %middle.2 = (f32[4096,256]{1,0:T(8,128)S(1)}, bf16[4096,256]{1,0:T(8,128)(2,1)S(1)}, f32[256,256]{1,0:T(8,128)S(1)}, f32[256,256]{1,0:T(8,128)S(1)}, f32[256,256]{1,0:T(8,128)S(1)}, /*index=5*/f32[256,256]{1,0:T(8,128)S(1)}) custom-call(s32[8]{0:T(128)S(1)} %stack.23.slots_ref, ...), custom_call_target="tpu_custom_call", output_to_operand_aliasing={{0}: (10, {})} | custom-call | tf_op jit(solution)/shard_map/middle/pallas_call | solution.py:351
  29.0 0.1 collective-permute-start.4
  29.1 3.4 %collective-permute-start.5 = (f32[256,256]{1,0:T(8,128)S(1)}, f32[256,256]{1,0:T(8,128)S(1)}, u32[]{:S(2)}, u32[]{:S(2)}) collective-permute-start(f32[256,256]{1,0:T(8,128)S(1)} %get-tuple-element.43), channel_id=1, source_target_pairs={{0,120},{8,16},{16,8},{24,32},{32,24},{40,48},{48,40},{56,64},{64,... | collective-permute-start | bytes 786440 | tf_op jit(solution)/shard_map/ppermute | solution.py:274
  32.5 0.0 collective-permute-start.6
  32.5 3.1 %collective-permute-start.7 = (f32[256,256]{1,0:T(8,128)S(1)}, f32[256,256]{1,0:T(8,128)S(1)}, u32[]{:S(2)}, u32[]{:S(2)}) collective-permute-start(f32[256,256]{1,0:T(8,128)S(1)} %get-tuple-element.45), channel_id=1, source_target_pairs={{0,7},{1,2},{2,1},{3,4},{4,3},{5,6},{6,5},{7,0},{8,15},{9,10},{10,... | collective-permute-start | bytes 786440 | tf_op jit(solution)/shard_map/ppermute | solution.py:274
  35.7 4.9 %own.2 = (f32[4096,256]{1,0:T(8,128)S(1)}, f32[8,128]{1,0:T(8,128)S(1)}) custom-call(s32[640]{0:T(1024)S(1)} %get-tuple-element.32.plan_ref, bf16[193,128,128]{2,1,0:T(8,128)(2,1)S(1)} %get-tuple-element.35.tiles_ref, bf16[4096,256]{1,0:T(8,128)(2,1)S(1)} %get-tuple-element.46.mixed_ref, f32[4096,256]{1,0:T(8,128)S(1)} %get-tuple-element.41.grad_ref.before_ref, ...), custom_call_target="tpu_custom_call" | custom-call | flops 10000000000 | bytes 16000000 | tf_op jit(solution)/shard_map/own/pallas_call | solution.py:339
  40.6 0.0 collective-permute-done.4.i0
  40.6 0.0 collective-permute-done.5.i1
  40.6 0.0 collective-permute-done.6.i2
  40.6 0.0 collective-permute-done.7.i3
  40.6 5.5 %middle.3 = (f32[4096,256]{1,0:T(8,128)S(1)}, bf16[4096,256]{1,0:T(8,128)(2,1)S(1)}, f32[256,256]{1,0:T(8,128)S(1)}, f32[256,256]{1,0:T(8,128)S(1)}, f32[256,256]{1,0:T(8,128)S(1)}, /*index=5*/f32[256,256]{1,0:T(8,128)S(1)}) custom-call(s32[8]{0:T(128)S(1)} %stack.23.slots_ref, ...), custom_call_target="tpu_custom_call", output_to_operand_aliasing={{0}: (10, {})} | custom-call | tf_op jit(solution)/shard_map/middle/pallas_call | solution.py:351
  46.1 0.1 collective-permute-start.8
  46.2 2.1 %collective-permute-start.9 = (f32[256,256]{1,0:T(8,128)S(1)}, f32[256,256]{1,0:T(8,128)S(1)}, u32[]{:S(2)}, u32[]{:S(2)}) collective-permute-start(f32[256,256]{1,0:T(8,128)S(1)} %get-tuple-element.50), channel_id=1, source_target_pairs={{0,120},{8,16},{16,8},{24,32},{32,24},{40,48},{48,40},{56,64},{64,... | collective-permute-start | bytes 786440 | tf_op jit(solution)/shard_map/ppermute | solution.py:274
  48.3 0.0 collective-permute-start.10
  48.3 3.2 %collective-permute-start.11 = (f32[256,256]{1,0:T(8,128)S(1)}, f32[256,256]{1,0:T(8,128)S(1)}, u32[]{:S(2)}, u32[]{:S(2)}) collective-permute-start(f32[256,256]{1,0:T(8,128)S(1)} %get-tuple-element.52), channel_id=1, source_target_pairs={{0,7},{1,2},{2,1},{3,4},{4,3},{5,6},{6,5},{7,0},{8,15},{9,10},{10,... | collective-permute-start | bytes 786440 | tf_op jit(solution)/shard_map/ppermute | solution.py:274
  51.5 5.1 %own.3 = (f32[4096,256]{1,0:T(8,128)S(1)}, f32[8,128]{1,0:T(8,128)S(1)}) custom-call(s32[640]{0:T(1024)S(1)} %get-tuple-element.32.plan_ref, bf16[193,128,128]{2,1,0:T(8,128)(2,1)S(1)} %get-tuple-element.35.tiles_ref, bf16[4096,256]{1,0:T(8,128)(2,1)S(1)} %get-tuple-element.55.mixed_ref, f32[4096,256]{1,0:T(8,128)S(1)} %get-tuple-element.41.grad_ref.before_ref, ...), custom_call_target="tpu_custom_call" | custom-call | flops 10000000000 | bytes 16000000 | tf_op jit(solution)/shard_map/own/pallas_call | solution.py:339
  56.5 0.0 collective-permute-done.8.i0
  56.6 0.0 collective-permute-done.9.i1
  56.6 0.0 collective-permute-done.10.i2
  56.6 0.0 collective-permute-done.11.i3
  56.6 4.0 %last.1 = (f32[4096,256]{1,0:T(8,128)}, f32[128,128]{1,0:T(8,128)S(1)}) custom-call(bf16[4096,1024]{1,0:T(8,128)(2,1)S(1)} %get-tuple-element.31.route_ref, f32[256,256]{1,0:T(8,128)S(1)} %collective-permute-done.8.i0, f32[256,256]{1,0:T(8,128)S(1)} %collective-permute-done.9.i1, f32[256,256]{1,0:T(8,128)S(1)} %collective-permute-done.10.i2, ...), custom_call_target="tpu_custom_call" | custom-call | tf_op jit(solution)/shard_map/last/pallas_call | solution.py:362
  60.5 15.9 %all_to_all.9 = f32[128,1,128]{2,1,0:T(1,128)S(1)} all-to-all(f32[128,1,128]{2,1,0:T(1,128)S(1)} %bitcast.8), channel_id=1, replica_groups=mesh['region'=16,'sub'=8] {'region','sub'}, dimensions={0} | all-to-all | bytes 131072 | tf_op jit(solution)/shard_map/all_to_all | solution.py:375
  76.4 0.2 reduce_sum.9
  76.6 0.5 add_sqrt_fusion
Async XLA Ops:
  9.0 14.5 %collective-permute-start = (f32[256,256]{1,0:T(8,128)S(1)}, f32[256,256]{1,0:T(8,128)S(1)}, u32[]{:S(2)}, u32[]{:S(2)}) collective-permute-start(f32[256,256]{1,0:T(8,128)S(1)} %get-tuple-element.36), channel_id=1, source_target_pairs={{0,8},{8,0},{16,24},{24,16},{32,40},{40,32},{48,56},{56,48},{64,72... | collective-permute-start | bytes 786440 | tf_op jit(solution)/shard_map/ppermute | solution.py:274
  11.1 12.4 %collective-permute-start.1 = (f32[256,256]{1,0:T(8,128)S(1)}, f32[256,256]{1,0:T(8,128)S(1)}, u32[]{:S(2)}, u32[]{:S(2)}) collective-permute-start(f32[256,256]{1,0:T(8,128)S(1)} %get-tuple-element.37), channel_id=1, source_target_pairs={{0,120},{8,16},{16,8},{24,32},{32,24},{40,48},{48,40},{56,64},{64,... | collective-permute-start | bytes 786440 | tf_op jit(solution)/shard_map/ppermute | solution.py:274
  15.8 7.7 %collective-permute-start.2 = (f32[256,256]{1,0:T(8,128)S(1)}, f32[256,256]{1,0:T(8,128)S(1)}, u32[]{:S(2)}, u32[]{:S(2)}) collective-permute-start(f32[256,256]{1,0:T(8,128)S(1)} %get-tuple-element.38), channel_id=1, source_target_pairs={{0,1},{1,0},{2,3},{3,2},{4,5},{5,4},{6,7},{7,6},{8,9},{9,8},{10,11... | collective-permute-start | bytes 786440 | tf_op jit(solution)/shard_map/ppermute | solution.py:274
  15.8 7.7 %collective-permute-start.3 = (f32[256,256]{1,0:T(8,128)S(1)}, f32[256,256]{1,0:T(8,128)S(1)}, u32[]{:S(2)}, u32[]{:S(2)}) collective-permute-start(f32[256,256]{1,0:T(8,128)S(1)} %get-tuple-element.39), channel_id=1, source_target_pairs={{0,7},{1,2},{2,1},{3,4},{4,3},{5,6},{6,5},{7,0},{8,15},{9,10},{10,... | collective-permute-start | bytes 786440 | tf_op jit(solution)/shard_map/ppermute | solution.py:274
  29.0 11.6 %collective-permute-start.4 = (f32[256,256]{1,0:T(8,128)S(1)}, f32[256,256]{1,0:T(8,128)S(1)}, u32[]{:S(2)}, u32[]{:S(2)}) collective-permute-start(f32[256,256]{1,0:T(8,128)S(1)} %get-tuple-element.42), channel_id=1, source_target_pairs={{0,8},{8,0},{16,24},{24,16},{32,40},{40,32},{48,56},{56,48},{64,72... | collective-permute-start | bytes 786440 | tf_op jit(solution)/shard_map/ppermute | solution.py:274
  29.1 11.5 %collective-permute-start.5 = (f32[256,256]{1,0:T(8,128)S(1)}, f32[256,256]{1,0:T(8,128)S(1)}, u32[]{:S(2)}, u32[]{:S(2)}) collective-permute-start(f32[256,256]{1,0:T(8,128)S(1)} %get-tuple-element.43), channel_id=1, source_target_pairs={{0,120},{8,16},{16,8},{24,32},{32,24},{40,48},{48,40},{56,64},{64,... | collective-permute-start | bytes 786440 | tf_op jit(solution)/shard_map/ppermute | solution.py:274
  32.5 8.1 %collective-permute-start.6 = (f32[256,256]{1,0:T(8,128)S(1)}, f32[256,256]{1,0:T(8,128)S(1)}, u32[]{:S(2)}, u32[]{:S(2)}) collective-permute-start(f32[256,256]{1,0:T(8,128)S(1)} %get-tuple-element.44), channel_id=1, source_target_pairs={{0,1},{1,0},{2,3},{3,2},{4,5},{5,4},{6,7},{7,6},{8,9},{9,8},{10,11... | collective-permute-start | bytes 786440 | tf_op jit(solution)/shard_map/ppermute | solution.py:274
  32.5 8.1 %collective-permute-start.7 = (f32[256,256]{1,0:T(8,128)S(1)}, f32[256,256]{1,0:T(8,128)S(1)}, u32[]{:S(2)}, u32[]{:S(2)}) collective-permute-start(f32[256,256]{1,0:T(8,128)S(1)} %get-tuple-element.45), channel_id=1, source_target_pairs={{0,7},{1,2},{2,1},{3,4},{4,3},{5,6},{6,5},{7,0},{8,15},{9,10},{10,... | collective-permute-start | bytes 786440 | tf_op jit(solution)/shard_map/ppermute | solution.py:274
  46.1 10.5 %collective-permute-start.8 = (f32[256,256]{1,0:T(8,128)S(1)}, f32[256,256]{1,0:T(8,128)S(1)}, u32[]{:S(2)}, u32[]{:S(2)}) collective-permute-start(f32[256,256]{1,0:T(8,128)S(1)} %get-tuple-element.49), channel_id=1, source_target_pairs={{0,8},{8,0},{16,24},{24,16},{32,40},{40,32},{48,56},{56,48},{64,72... | collective-permute-start | bytes 786440 | tf_op jit(solution)/shard_map/ppermute | solution.py:274
  46.2 10.4 %collective-permute-start.9 = (f32[256,256]{1,0:T(8,128)S(1)}, f32[256,256]{1,0:T(8,128)S(1)}, u32[]{:S(2)}, u32[]{:S(2)}) collective-permute-start(f32[256,256]{1,0:T(8,128)S(1)} %get-tuple-element.50), channel_id=1, source_target_pairs={{0,120},{8,16},{16,8},{24,32},{32,24},{40,48},{48,40},{56,64},{64,... | collective-permute-start | bytes 786440 | tf_op jit(solution)/shard_map/ppermute | solution.py:274
  48.3 8.3 %collective-permute-start.10 = (f32[256,256]{1,0:T(8,128)S(1)}, f32[256,256]{1,0:T(8,128)S(1)}, u32[]{:S(2)}, u32[]{:S(2)}) collective-permute-start(f32[256,256]{1,0:T(8,128)S(1)} %get-tuple-element.51), channel_id=1, source_target_pairs={{0,1},{1,0},{2,3},{3,2},{4,5},{5,4},{6,7},{7,6},{8,9},{9,8},{10,11... | collective-permute-start | bytes 786440 | tf_op jit(solution)/shard_map/ppermute | solution.py:274
  48.3 8.3 %collective-permute-start.11 = (f32[256,256]{1,0:T(8,128)S(1)}, f32[256,256]{1,0:T(8,128)S(1)}, u32[]{:S(2)}, u32[]{:S(2)}) collective-permute-start(f32[256,256]{1,0:T(8,128)S(1)} %get-tuple-element.52), channel_id=1, source_target_pairs={{0,7},{1,2},{2,1},{3,4},{4,3},{5,6},{6,5},{7,0},{8,15},{9,10},{10,... | collective-permute-start | bytes 786440 | tf_op jit(solution)/shard_map/ppermute | solution.py:274

commit v3 on v2

--- a/solution.py
+++ b/solution.py
@@ -10,6 +10,7 @@
 ITERS = 3
 B = 128
 LOAD = 1024
+STORE = 1024
 CHUNK = 2048
 OWN_GROUP = 16
 GHOST_GROUP = 8
@@ -116,9 +117,13 @@
         at = pl.ds(p * LOAD, LOAD)
         copies.append(pltpu.make_async_copy(state_hbm.at[at], state_ref.at[at], sems.at[4 + 2 * p]))
         copies.append(pltpu.make_async_copy(grad_hbm.at[at], grad_ref.at[at], sems.at[5 + 2 * p]))
-    copies.append(
-        pltpu.make_async_copy(tiles_hbm, tiles_ref.at[pl.ds(0, tile_count)], sems.at[4 + 2 * parts])
-    )
+    tile_parts = 4
+    some = tile_count // tile_parts
+    for q in range(tile_parts):
+        at = pl.ds(q * some, some)
+        copies.append(
+            pltpu.make_async_copy(tiles_hbm.at[at], tiles_ref.at[at], sems.at[4 + 2 * parts + q])
+        )
     for copy in copies:
         copy.start()
     tiles_ref[tile_count] = jnp.zeros((B, B), jnp.bfloat16)
@@ -130,27 +135,33 @@
     steps = tile_count // 3
     band = row_count // steps
 
+    agent = lax.broadcasted_iota(jnp.int32, (band, size), 0)
+    target_rows = [targets_ref[pl.ds(slots_ref[4 + slot], 1), :] for slot in range(4)]
+
     def place(g, counts):
         ghost_count, own_count = counts
+        cols = [cols_ref[g * 3 + u] for u in range(3)]
+        entries = [rows_ref[g * 3 + u] * 256 + (g * 3 + u) for u in range(3)]
+        others = [waiting_ref[col] for col in cols]
+        lefts = []
         for u in range(3):
-            t = g * 3 + u
-            col = cols_ref[t]
-            entry = t + rows_ref[t] * 256
-            other = waiting_ref[col]
-            paired = (other >= 0).astype(jnp.int32)
-            is_ghost = (col >= own_blocks).astype(jnp.int32)
+            for v in range(u):
+                others[u] = jnp.where(cols[u] == cols[v], lefts[v], others[u])
+            lefts.append(jnp.where(others[u] >= 0, -1, entries[u]))
+        for u in range(3):
+            paired = (others[u] >= 0).astype(jnp.int32)
+            is_ghost = (cols[u] >= own_blocks).astype(jnp.int32)
             at = jnp.where(is_ghost == 1, ghost_count, OWN_AT + own_count)
-            plan_ref[at] = entry + col * 65536
-            plan_ref[at + SECOND] = other
-            waiting_ref[col] = jnp.where(paired == 1, -1, entry)
+            plan_ref[at] = entries[u] + cols[u] * 65536
+            plan_ref[at + SECOND] = others[u]
             ghost_count = ghost_count + is_ghost * paired
             own_count = own_count + (1 - is_ghost) * paired
+        for u in range(3):
+            waiting_ref[cols[u]] = lefts[u]
         rows = pl.ds(pl.multiple_of(g * band, band), band)
-        agent = lax.broadcasted_iota(jnp.int32, (band, size), 0) + g * band
         for slot in range(4):
-            target = targets_ref[pl.ds(slots_ref[4 + slot], 1), :]
             route_ref[rows, slot * size:(slot + 1) * size] = jnp.where(
-                agent == target, 1.0, 0.0
+                agent == target_rows[slot] - g * band, 1.0, 0.0
             ).astype(jnp.bfloat16)
         return ghost_count, own_count
 
@@ -177,7 +188,8 @@
         copies[5 + 2 * p].wait()
         at = pl.ds(p * LOAD, LOAD)
         mix(grad_ref[at, :], state_ref, weight_ref, mixed_ref, at)
-    copies[-1].wait()
+    for copy in copies[-tile_parts:]:
+        copy.wait()
     ghosts(plan_ref, slots_ref, tiles_ref, mixed_ref, ghost_ref, (g0, g1, g2, g3), own_blocks)
 
 
@@ -227,29 +239,33 @@
 
 def last_kernel(
     route_ref, i0, i1, i2, i3, before_ref, change0_ref, change1_ref, partial_ref,
-    adjoint_hbm, sums_ref, incoming_ref, adjoint_ref, sems,
+    adjoint_hbm, sums_ref, incoming_ref, adjoint_ref, change_ref, sems,
 ):
     gather_incoming((i0, i1, i2, i3), incoming_ref)
     row_count = partial_ref.shape[0]
-    change = jnp.zeros((8, 128), jnp.float32)
-    copies = []
-    for p in range(row_count // LOAD):
-        rows = pl.ds(p * LOAD, LOAD)
+    change_ref[...] = jnp.zeros_like(change_ref)
+
+    def store(i):
+        rows = pl.ds(pl.multiple_of(i * STORE, STORE), STORE)
+        return pltpu.make_async_copy(adjoint_ref.at[rows], adjoint_hbm.at[rows], sems.at[i])
+
+    @pl.loop(0, row_count // STORE)
+    def _(i):
+        rows = pl.ds(pl.multiple_of(i * STORE, STORE), STORE)
         adjoint = partial_ref[rows, :] + jnp.dot(
             route_ref[rows, :], incoming_ref[...], preferred_element_type=jnp.float32
         )
         adjoint_ref[rows, :] = adjoint
-        copies.append(pltpu.make_async_copy(adjoint_ref.at[rows], adjoint_hbm.at[rows], sems.at[p]))
-        copies[-1].start()
-        change += squares(adjoint - before_ref[rows, :])
+        store(i).start()
+        change_ref[...] += squares(adjoint - before_ref[rows, :])
 
     lane = lax.broadcasted_iota(jnp.int32, sums_ref.shape, 1)
     sums = jnp.zeros(sums_ref.shape, jnp.float32)
-    for i, value in enumerate((change0_ref[...], change1_ref[...], change)):
+    for i, value in enumerate((change0_ref[...], change1_ref[...], change_ref[...])):
         sums = jnp.where(lane == i, jnp.sum(value), sums)
     sums_ref[...] = sums
-    for copy in copies:
-        copy.wait()
+    for i in range(row_count // STORE):
+        store(i).wait()
 
 
 def local(state, grad_out, weight, tiles, tile_row, tile_col, send_rows):
@@ -265,8 +281,8 @@
     region_odd = lax.axis_index("region") % 2
     sub_odd = lax.axis_index("sub") % 2
     slots = jnp.stack(
-        [region_odd, 1 - region_odd, 2 + sub_odd, 3 - sub_odd,
-         1 - region_odd, region_odd, 3 - sub_odd, 2 + sub_odd]
+        [1 - region_odd, region_odd, 3 - sub_odd, 2 + sub_odd,
+         region_odd, 1 - region_odd, 2 + sub_odd, 3 - sub_odd]
     ).astype(i32)
 
     def swap(value, axis, count, odd):
@@ -275,10 +291,10 @@
 
     def exchange(outgoing):
         return (
-            swap(outgoing[0], "region", region_count, 0),
-            swap(outgoing[1], "region", region_count, 1),
-            swap(outgoing[2], "sub", sub_count, 0),
-            swap(outgoing[3], "sub", sub_count, 1),
+            swap(outgoing[0], "region", region_count, 1),
+            swap(outgoing[1], "region", region_count, 0),
+            swap(outgoing[2], "sub", sub_count, 1),
+            swap(outgoing[3], "sub", sub_count, 0),
         )
 
     params = pltpu.CompilerParams(vmem_limit_bytes=VMEM_LIMIT)
@@ -311,7 +327,7 @@
             SMEM((128,), i32),
             VMEM((4, ghost_count), i32),
             ghost_scratch,
-            pltpu.SemaphoreType.DMA((5 + 2 * parts,)),
+            pltpu.SemaphoreType.DMA((8 + 2 * parts,)),
         ],
         compiler_params=params,
         name="first",
@@ -367,7 +383,12 @@
                     pltpu.HBM((row_count, feature_count), f32),
                     VMEM((region_count * sub_count, 128), f32),
                 ),
-                scratch_shapes=[incoming_scratch, agents_f32, pltpu.SemaphoreType.DMA((parts,))],
+                scratch_shapes=[
+                    incoming_scratch,
+                    agents_f32,
+                    VMEM((8, 128), f32),
+                    pltpu.SemaphoreType.DMA((row_count // STORE,)),
+                ],
                 compiler_params=params,
                 name="last",
             )(route, *incoming, kept(before), *changes, kept(partial))

time: 77.7 us -> 77.4 us (level); the launches traced: 77.1 us -> 77.8 us
  starting transfers between devices: 22 us -> 19.1 us
  waiting for transfers between devices: 0.03 us -> 2.82 us
  blocking collectives: 15.9 us -> 17.5 us
    ppermute x12, starting transfers between devices: 22 us -> 19.1 us  [swap(): return lax.ppermute(value, axis, list(enumerate(partner)))]
    ppermute x12, waiting for transfers between devices: 0.03 us -> 2.82 us  [swap(): return lax.ppermute(value, axis, list(enumerate(partner)))]
    all_to_all x1, blocking collectives: 15.9 us -> 17.5 us  [local(): sums = lax.all_to_all(sums, ('region', 'sub'), 0, 0, tiled=True)]
  transfers between devices with their start and end apart: 12 -> 12, of which waited for: 0 -> 3; matrix products, arithmetic and copies ran while one was open for 0% -> 0% of each run, Pallas kernels for 19% -> 19%
where the time goes in v3:
time: 77.4 us; the launch traced here: 77.8 us
  Pallas kernels  36.9 us (48%)
  starting transfers between devices  19.1 us (25%)
  blocking collectives  17.5 us (23%)
  waiting for transfers between devices  2.82 us (4%)
    ppermute x12, starting transfers between devices, swap(): return lax.ppermute(value, axis, list(enumerate(partner)))  19.1 us
    all_to_all x1, blocking collectives, local(): sums = lax.all_to_all(sums, ('region', 'sub'), 0, 0, tiled=True)  17.5 us
    pallas_call x2, Pallas kernels, local(): pl.pallas_call(functools.partial(middle_kernel, own_blocks), in_specs=sme...  10.9 us
    pallas_call x2, Pallas kernels, local(): pl.pallas_call(own_kernel, in_specs=smem_specs(1) + vmem_specs(5), out_sp...  9.98 us
    pallas_call x1, Pallas kernels, local(): pl.pallas_call(functools.partial(first_kernel, own_blocks), in_specs=smem...  7.5 us
    pallas_call x1, Pallas kernels, local(): pl.pallas_call(first_own_kernel, in_specs=smem_specs(1) + vmem_specs(3),...  4.52 us
    pallas_call x1, Pallas kernels, local(): pl.pallas_call(last_kernel, in_specs=vmem_specs(9), out_specs=(pl.BlockSp...  4 us
    ppermute x12, waiting for transfers between devices, swap(): return lax.ppermute(value, axis, list(enumerate(partner)))  2.82 us
  transfers between devices with their start and end apart: 12, of which 3 were waited for; matrix products, arithmetic and copies ran while one was open for 0% of the time, Pallas kernels for 19%

profile of v3, /device:TPU:0, one launch (start us, length us, event | category | flops | bytes accessed | tf_op | source)
XLA Modules:
  0.0 77.8 jit_solution(2016238660456084082)
XLA Ops:
  0.6 0.1 stack.23.slots_ref
  0.7 7.5 %first.1 = (bf16[256,256]{1,0:T(8,128)(2,1)S(1)}, bf16[4096,256]{1,0:T(8,128)(2,1)S(1)}, f32[4096,256]{1,0:T(8,128)S(1)}, bf16[193,128,128]{2,1,0:T(8,128)(2,1)S...) custom-call(s32[8]{0:T(128)S(1)} %stack.23.slots_ref, ...), custom_call_target="tpu_custom_call" | custom-call | tf_op jit(solution)/shard_map/first/pallas_call | solution.py:310
  8.2 6.4 %collective-permute-start = (f32[256,256]{1,0:T(8,128)S(1)}, f32[256,256]{1,0:T(8,128)S(1)}, u32[]{:S(2)}, u32[]{:S(2)}) collective-permute-start(f32[256,256]{1,0:T(8,128)S(1)} %get-tuple-element.36), channel_id=1, source_target_pairs={{0,120},{8,16},{16,8},{24,32},{32,24},{40,48},{48,40},{56,64},{64,... | collective-permute-start | bytes 786440 | tf_op jit(solution)/shard_map/ppermute | solution.py:290
  14.6 0.0 collective-permute-start.1
  14.6 2.2 %collective-permute-start.2 = (f32[256,256]{1,0:T(8,128)S(1)}, f32[256,256]{1,0:T(8,128)S(1)}, u32[]{:S(2)}, u32[]{:S(2)}) collective-permute-start(f32[256,256]{1,0:T(8,128)S(1)} %get-tuple-element.38), channel_id=1, source_target_pairs={{0,7},{1,2},{2,1},{3,4},{4,3},{5,6},{6,5},{7,0},{8,15},{9,10},{10,... | collective-permute-start | bytes 786440 | tf_op jit(solution)/shard_map/ppermute | solution.py:290
  16.8 0.0 collective-permute-start.3
  16.8 4.5 %first_own.1.partial_ref = f32[4096,256]{1,0:T(8,128)S(1)} custom-call(s32[640]{0:T(1024)S(1)} %get-tuple-element.32.plan_ref, bf16[193,128,128]{2,1,0:T(8,128)(2,1)S(1)} %get-tuple-element.35.tiles_ref, bf16[4096,256]{1,0:T(8,128)(2,1)S(1)} %get-tuple-element.40.mixed_ref, f32[4096,256]{1,0:T(8,128)S(1)} %get-tuple-element.41.grad_ref.before_ref), custom_call_target="tpu_custom_call" | custom-call | flops 10000000000 | bytes 16000000 | tf_op jit(solution)/shard_map/first_own/pallas_call | solution.py:345
  21.3 0.0 collective-permute-done.i0
  21.4 1.0 %collective-permute-done.1.i1 = f32[256,256]{1,0:T(8,128)S(1)} collective-permute-done((f32[256,256]{1,0:T(8,128)S(1)}, f32[256,256]{1,0:T(8,128)S(1)}, u32[]{:S(2)}, u32[]{:S(2)}) %collective-permute-start.1) | collective-permute-done | bytes 262176 | tf_op jit(solution)/shard_map/ppermute | solution.py:290
  22.4 0.0 collective-permute-done.2.i2
  22.4 0.0 collective-permute-done.3.i3
  22.4 5.5 %middle.2 = (f32[4096,256]{1,0:T(8,128)S(1)}, bf16[4096,256]{1,0:T(8,128)(2,1)S(1)}, f32[256,256]{1,0:T(8,128)S(1)}, f32[256,256]{1,0:T(8,128)S(1)}, f32[256,256]{1,0:T(8,128)S(1)}, /*index=5*/f32[256,256]{1,0:T(8,128)S(1)}) custom-call(s32[8]{0:T(128)S(1)} %stack.23.slots_ref, ...), custom_call_target="tpu_custom_call", output_to_operand_aliasing={{0}: (10, {})} | custom-call | tf_op jit(solution)/shard_map/middle/pallas_call | solution.py:367
  27.9 3.7 %collective-permute-start.4 = (f32[256,256]{1,0:T(8,128)S(1)}, f32[256,256]{1,0:T(8,128)S(1)}, u32[]{:S(2)}, u32[]{:S(2)}) collective-permute-start(f32[256,256]{1,0:T(8,128)S(1)} %get-tuple-element.42), channel_id=1, source_target_pairs={{0,120},{8,16},{16,8},{24,32},{32,24},{40,48},{48,40},{56,64},{64,... | collective-permute-start | bytes 786440 | tf_op jit(solution)/shard_map/ppermute | solution.py:290
  31.6 0.0 collective-permute-start.5
  31.6 1.3 %collective-permute-start.6 = (f32[256,256]{1,0:T(8,128)S(1)}, f32[256,256]{1,0:T(8,128)S(1)}, u32[]{:S(2)}, u32[]{:S(2)}) collective-permute-start(f32[256,256]{1,0:T(8,128)S(1)} %get-tuple-element.44), channel_id=1, source_target_pairs={{0,7},{1,2},{2,1},{3,4},{4,3},{5,6},{6,5},{7,0},{8,15},{9,10},{10,... | collective-permute-start | bytes 786440 | tf_op jit(solution)/shard_map/ppermute | solution.py:290
  32.9 0.7 collective-permute-start.7
  33.6 4.9 %own.2 = (f32[4096,256]{1,0:T(8,128)S(1)}, f32[8,128]{1,0:T(8,128)S(1)}) custom-call(s32[640]{0:T(1024)S(1)} %get-tuple-element.32.plan_ref, bf16[193,128,128]{2,1,0:T(8,128)(2,1)S(1)} %get-tuple-element.35.tiles_ref, bf16[4096,256]{1,0:T(8,128)(2,1)S(1)} %get-tuple-element.46.mixed_ref, f32[4096,256]{1,0:T(8,128)S(1)} %get-tuple-element.41.grad_ref.before_ref, ...), custom_call_target="tpu_custom_call" | custom-call | flops 10000000000 | bytes 16000000 | tf_op jit(solution)/shard_map/own/pallas_call | solution.py:355
  38.5 0.5 collective-permute-done.4.i0
  39.0 0.0 collective-permute-done.5.i1
  39.0 0.0 collective-permute-done.6.i2
  39.0 0.0 collective-permute-done.7.i3
  39.0 5.5 %middle.3 = (f32[4096,256]{1,0:T(8,128)S(1)}, bf16[4096,256]{1,0:T(8,128)(2,1)S(1)}, f32[256,256]{1,0:T(8,128)S(1)}, f32[256,256]{1,0:T(8,128)S(1)}, f32[256,256]{1,0:T(8,128)S(1)}, /*index=5*/f32[256,256]{1,0:T(8,128)S(1)}) custom-call(s32[8]{0:T(128)S(1)} %stack.23.slots_ref, ...), custom_call_target="tpu_custom_call", output_to_operand_aliasing={{0}: (10, {})} | custom-call | tf_op jit(solution)/shard_map/middle/pallas_call | solution.py:367
  44.4 3.2 %collective-permute-start.8 = (f32[256,256]{1,0:T(8,128)S(1)}, f32[256,256]{1,0:T(8,128)S(1)}, u32[]{:S(2)}, u32[]{:S(2)}) collective-permute-start(f32[256,256]{1,0:T(8,128)S(1)} %get-tuple-element.49), channel_id=1, source_target_pairs={{0,120},{8,16},{16,8},{24,32},{32,24},{40,48},{48,40},{56,64},{64,... | collective-permute-start | bytes 786440 | tf_op jit(solution)/shard_map/ppermute | solution.py:290
  47.6 0.0 collective-permute-start.9
  47.6 0.4 collective-permute-start.10
  48.0 1.3 %collective-permute-start.11 = (f32[256,256]{1,0:T(8,128)S(1)}, f32[256,256]{1,0:T(8,128)S(1)}, u32[]{:S(2)}, u32[]{:S(2)}) collective-permute-start(f32[256,256]{1,0:T(8,128)S(1)} %get-tuple-element.52), channel_id=1, source_target_pairs={{0,1},{1,0},{2,3},{3,2},{4,5},{5,4},{6,7},{7,6},{8,9},{9,8},{10,11... | collective-permute-start | bytes 786440 | tf_op jit(solution)/shard_map/ppermute | solution.py:290
  49.3 5.1 %own.3 = (f32[4096,256]{1,0:T(8,128)S(1)}, f32[8,128]{1,0:T(8,128)S(1)}) custom-call(s32[640]{0:T(1024)S(1)} %get-tuple-element.32.plan_ref, bf16[193,128,128]{2,1,0:T(8,128)(2,1)S(1)} %get-tuple-element.35.tiles_ref, bf16[4096,256]{1,0:T(8,128)(2,1)S(1)} %get-tuple-element.55.mixed_ref, f32[4096,256]{1,0:T(8,128)S(1)} %get-tuple-element.41.grad_ref.before_ref, ...), custom_call_target="tpu_custom_call" | custom-call | flops 10000000000 | bytes 16000000 | tf_op jit(solution)/shard_map/own/pallas_call | solution.py:355
  54.3 1.3 %collective-permute-done.8.i0 = f32[256,256]{1,0:T(8,128)S(1)} collective-permute-done((f32[256,256]{1,0:T(8,128)S(1)}, f32[256,256]{1,0:T(8,128)S(1)}, u32[]{:S(2)}, u32[]{:S(2)}) %collective-permute-start.8) | collective-permute-done | bytes 262176 | tf_op jit(solution)/shard_map/ppermute | solution.py:290
  55.6 0.0 collective-permute-done.9.i1
  55.6 0.0 collective-permute-done.10.i2
  55.6 0.0 collective-permute-done.11.i3
  55.6 4.0 %last.1 = (f32[4096,256]{1,0:T(8,128)}, f32[128,128]{1,0:T(8,128)S(1)}) custom-call(bf16[4096,1024]{1,0:T(8,128)(2,1)S(1)} %get-tuple-element.31.route_ref, f32[256,256]{1,0:T(8,128)S(1)} %collective-permute-done.8.i0, f32[256,256]{1,0:T(8,128)S(1)} %collective-permute-done.9.i1, f32[256,256]{1,0:T(8,128)S(1)} %collective-permute-done.10.i2, ...), custom_call_target="tpu_custom_call" | custom-call | tf_op jit(solution)/shard_map/last/pallas_call | solution.py:378
  59.7 17.5 %all_to_all.9 = f32[128,1,128]{2,1,0:T(1,128)S(1)} all-to-all(f32[128,1,128]{2,1,0:T(1,128)S(1)} %bitcast.8), channel_id=1, replica_groups=mesh['region'=16,'sub'=8] {'region','sub'}, dimensions={0} | all-to-all | bytes 131072 | tf_op jit(solution)/shard_map/all_to_all | solution.py:396
  77.1 0.2 reduce_sum.9
  77.3 0.5 add_sqrt_fusion
Async XLA Ops:
  8.2 13.1 %collective-permute-start = (f32[256,256]{1,0:T(8,128)S(1)}, f32[256,256]{1,0:T(8,128)S(1)}, u32[]{:S(2)}, u32[]{:S(2)}) collective-permute-start(f32[256,256]{1,0:T(8,128)S(1)} %get-tuple-element.36), channel_id=1, source_target_pairs={{0,120},{8,16},{16,8},{24,32},{32,24},{40,48},{48,40},{56,64},{64,... | collective-permute-start | bytes 786440 | tf_op jit(solution)/shard_map/ppermute | solution.py:290
  14.6 7.8 %collective-permute-start.1 = (f32[256,256]{1,0:T(8,128)S(1)}, f32[256,256]{1,0:T(8,128)S(1)}, u32[]{:S(2)}, u32[]{:S(2)}) collective-permute-start(f32[256,256]{1,0:T(8,128)S(1)} %get-tuple-element.37), channel_id=1, source_target_pairs={{0,8},{8,0},{16,24},{24,16},{32,40},{40,32},{48,56},{56,48},{64,72... | collective-permute-start | bytes 786440 | tf_op jit(solution)/shard_map/ppermute | solution.py:290
  14.6 7.8 %collective-permute-start.2 = (f32[256,256]{1,0:T(8,128)S(1)}, f32[256,256]{1,0:T(8,128)S(1)}, u32[]{:S(2)}, u32[]{:S(2)}) collective-permute-start(f32[256,256]{1,0:T(8,128)S(1)} %get-tuple-element.38), channel_id=1, source_target_pairs={{0,7},{1,2},{2,1},{3,4},{4,3},{5,6},{6,5},{7,0},{8,15},{9,10},{10,... | collective-permute-start | bytes 786440 | tf_op jit(solution)/shard_map/ppermute | solution.py:290
  16.8 5.6 %collective-permute-start.3 = (f32[256,256]{1,0:T(8,128)S(1)}, f32[256,256]{1,0:T(8,128)S(1)}, u32[]{:S(2)}, u32[]{:S(2)}) collective-permute-start(f32[256,256]{1,0:T(8,128)S(1)} %get-tuple-element.39), channel_id=1, source_target_pairs={{0,1},{1,0},{2,3},{3,2},{4,5},{5,4},{6,7},{7,6},{8,9},{9,8},{10,11... | collective-permute-start | bytes 786440 | tf_op jit(solution)/shard_map/ppermute | solution.py:290
  27.9 11.1 %collective-permute-start.4 = (f32[256,256]{1,0:T(8,128)S(1)}, f32[256,256]{1,0:T(8,128)S(1)}, u32[]{:S(2)}, u32[]{:S(2)}) collective-permute-start(f32[256,256]{1,0:T(8,128)S(1)} %get-tuple-element.42), channel_id=1, source_target_pairs={{0,120},{8,16},{16,8},{24,32},{32,24},{40,48},{48,40},{56,64},{64,... | collective-permute-start | bytes 786440 | tf_op jit(solution)/shard_map/ppermute | solution.py:290
  31.6 7.4 %collective-permute-start.5 = (f32[256,256]{1,0:T(8,128)S(1)}, f32[256,256]{1,0:T(8,128)S(1)}, u32[]{:S(2)}, u32[]{:S(2)}) collective-permute-start(f32[256,256]{1,0:T(8,128)S(1)} %get-tuple-element.43), channel_id=1, source_target_pairs={{0,8},{8,0},{16,24},{24,16},{32,40},{40,32},{48,56},{56,48},{64,72... | collective-permute-start | bytes 786440 | tf_op jit(solution)/shard_map/ppermute | solution.py:290
  31.6 7.4 %collective-permute-start.6 = (f32[256,256]{1,0:T(8,128)S(1)}, f32[256,256]{1,0:T(8,128)S(1)}, u32[]{:S(2)}, u32[]{:S(2)}) collective-permute-start(f32[256,256]{1,0:T(8,128)S(1)} %get-tuple-element.44), channel_id=1, source_target_pairs={{0,7},{1,2},{2,1},{3,4},{4,3},{5,6},{6,5},{7,0},{8,15},{9,10},{10,... | collective-permute-start | bytes 786440 | tf_op jit(solution)/shard_map/ppermute | solution.py:290
  32.9 6.1 %collective-permute-start.7 = (f32[256,256]{1,0:T(8,128)S(1)}, f32[256,256]{1,0:T(8,128)S(1)}, u32[]{:S(2)}, u32[]{:S(2)}) collective-permute-start(f32[256,256]{1,0:T(8,128)S(1)} %get-tuple-element.45), channel_id=1, source_target_pairs={{0,1},{1,0},{2,3},{3,2},{4,5},{5,4},{6,7},{7,6},{8,9},{9,8},{10,11... | collective-permute-start | bytes 786440 | tf_op jit(solution)/shard_map/ppermute | solution.py:290
  44.4 11.2 %collective-permute-start.8 = (f32[256,256]{1,0:T(8,128)S(1)}, f32[256,256]{1,0:T(8,128)S(1)}, u32[]{:S(2)}, u32[]{:S(2)}) collective-permute-start(f32[256,256]{1,0:T(8,128)S(1)} %get-tuple-element.49), channel_id=1, source_target_pairs={{0,120},{8,16},{16,8},{24,32},{32,24},{40,48},{48,40},{56,64},{64,... | collective-permute-start | bytes 786440 | tf_op jit(solution)/shard_map/ppermute | solution.py:290
  47.6 8.0 %collective-permute-start.9 = (f32[256,256]{1,0:T(8,128)S(1)}, f32[256,256]{1,0:T(8,128)S(1)}, u32[]{:S(2)}, u32[]{:S(2)}) collective-permute-start(f32[256,256]{1,0:T(8,128)S(1)} %get-tuple-element.50), channel_id=1, source_target_pairs={{0,8},{8,0},{16,24},{24,16},{32,40},{40,32},{48,56},{56,48},{64,72... | collective-permute-start | bytes 786440 | tf_op jit(solution)/shard_map/ppermute | solution.py:290
  47.6 8.0 %collective-permute-start.10 = (f32[256,256]{1,0:T(8,128)S(1)}, f32[256,256]{1,0:T(8,128)S(1)}, u32[]{:S(2)}, u32[]{:S(2)}) collective-permute-start(f32[256,256]{1,0:T(8,128)S(1)} %get-tuple-element.51), channel_id=1, source_target_pairs={{0,7},{1,2},{2,1},{3,4},{4,3},{5,6},{6,5},{7,0},{8,15},{9,10},{10,... | collective-permute-start | bytes 786440 | tf_op jit(solution)/shard_map/ppermute | solution.py:290
  48.0 7.6 %collective-permute-start.11 = (f32[256,256]{1,0:T(8,128)S(1)}, f32[256,256]{1,0:T(8,128)S(1)}, u32[]{:S(2)}, u32[]{:S(2)}) collective-permute-start(f32[256,256]{1,0:T(8,128)S(1)} %get-tuple-element.52), channel_id=1, source_target_pairs={{0,1},{1,0},{2,3},{3,2},{4,5},{5,4},{6,7},{7,6},{8,9},{9,8},{10,11... | collective-permute-start | bytes 786440 | tf_op jit(solution)/shard_map/ppermute | solution.py:290

commit v4 on v3

--- a/solution.py
+++ b/solution.py
@@ -13,7 +13,7 @@
 STORE = 1024
 CHUNK = 2048
 OWN_GROUP = 16
-GHOST_GROUP = 8
+GHOST_GROUP = 12
 SECOND = 128
 OWN_AT = 256
 COUNTS_AT = 512

time: 77.4 us -> 76.7 us (level); the launches traced: 77.8 us -> 75.5 us
  blocking collectives: 17.5 us -> 14.7 us
  waiting for transfers between devices: 2.82 us -> 5.4 us
  starting transfers between devices: 19.1 us -> 17.4 us
    all_to_all x1, blocking collectives: 17.5 us -> 14.7 us  [local(): sums = lax.all_to_all(sums, ('region', 'sub'), 0, 0, tiled=True)]
    ppermute x12, waiting for transfers between devices: 2.82 us -> 5.4 us  [swap(): return lax.ppermute(value, axis, list(enumerate(partner)))]
    ppermute x12, starting transfers between devices: 19.1 us -> 17.4 us  [swap(): return lax.ppermute(value, axis, list(enumerate(partner)))]
  transfers between devices with their start and end apart: 12 -> 12, of which waited for: 3 -> 6; matrix products, arithmetic and copies ran while one was open for 0% -> 0% of each run, Pallas kernels for 19% -> 19%
where the time goes in v4:
time: 76.7 us; the launch traced here: 75.5 us
  Pallas kernels  36.5 us (48%)
  starting transfers between devices  17.4 us (23%)
  blocking collectives  14.7 us (19%)
  waiting for transfers between devices  5.4 us (7%)
    ppermute x12, starting transfers between devices, swap(): return lax.ppermute(value, axis, list(enumerate(partner)))  17.4 us
    all_to_all x1, blocking collectives, local(): sums = lax.all_to_all(sums, ('region', 'sub'), 0, 0, tiled=True)  14.7 us
    pallas_call x2, Pallas kernels, local(): pl.pallas_call(functools.partial(middle_kernel, own_blocks), in_specs=sme...  10.6 us
    pallas_call x2, Pallas kernels, local(): pl.pallas_call(own_kernel, in_specs=smem_specs(1) + vmem_specs(5), out_sp...  9.98 us
    pallas_call x1, Pallas kernels, local(): pl.pallas_call(functools.partial(first_kernel, own_blocks), in_specs=smem...  7.38 us
    ppermute x12, waiting for transfers between devices, swap(): return lax.ppermute(value, axis, list(enumerate(partner)))  5.4 us
    pallas_call x1, Pallas kernels, local(): pl.pallas_call(first_own_kernel, in_specs=smem_specs(1) + vmem_specs(3),...  4.52 us
    pallas_call x1, Pallas kernels, local(): pl.pallas_call(last_kernel, in_specs=vmem_specs(9), out_specs=(pl.BlockSp...  4 us
  transfers between devices with their start and end apart: 12, of which 6 were waited for; matrix products, arithmetic and copies ran while one was open for 0% of the time, Pallas kernels for 19%

profile of v4, /device:TPU:0, one launch (start us, length us, event | category | flops | bytes accessed | tf_op | source)
XLA Modules:
  0.0 75.5 jit_solution(13036880020549354150)
XLA Ops:
  0.6 0.1 stack.23.slots_ref
  0.7 7.4 %first.1 = (bf16[256,256]{1,0:T(8,128)(2,1)S(1)}, bf16[4096,256]{1,0:T(8,128)(2,1)S(1)}, f32[4096,256]{1,0:T(8,128)S(1)}, bf16[193,128,128]{2,1,0:T(8,128)(2,1)S...) custom-call(s32[8]{0:T(128)S(1)} %stack.23.slots_ref, ...), custom_call_target="tpu_custom_call" | custom-call | tf_op jit(solution)/shard_map/first/pallas_call | solution.py:310
  8.1 6.4 %collective-permute-start = (f32[256,256]{1,0:T(8,128)S(1)}, f32[256,256]{1,0:T(8,128)S(1)}, u32[]{:S(2)}, u32[]{:S(2)}) collective-permute-start(f32[256,256]{1,0:T(8,128)S(1)} %get-tuple-element.36), channel_id=1, source_target_pairs={{0,120},{8,16},{16,8},{24,32},{32,24},{40,48},{48,40},{56,64},{64,... | collective-permute-start | bytes 786440 | tf_op jit(solution)/shard_map/ppermute | solution.py:290
  14.5 0.0 collective-permute-start.1
  14.5 2.2 %collective-permute-start.2 = (f32[256,256]{1,0:T(8,128)S(1)}, f32[256,256]{1,0:T(8,128)S(1)}, u32[]{:S(2)}, u32[]{:S(2)}) collective-permute-start(f32[256,256]{1,0:T(8,128)S(1)} %get-tuple-element.38), channel_id=1, source_target_pairs={{0,7},{1,2},{2,1},{3,4},{4,3},{5,6},{6,5},{7,0},{8,15},{9,10},{10,... | collective-permute-start | bytes 786440 | tf_op jit(solution)/shard_map/ppermute | solution.py:290
  16.7 0.0 collective-permute-start.3
  16.7 4.5 %first_own.1.partial_ref = f32[4096,256]{1,0:T(8,128)S(1)} custom-call(s32[640]{0:T(1024)S(1)} %get-tuple-element.32.plan_ref, bf16[193,128,128]{2,1,0:T(8,128)(2,1)S(1)} %get-tuple-element.35.tiles_ref, bf16[4096,256]{1,0:T(8,128)(2,1)S(1)} %get-tuple-element.40.mixed_ref, f32[4096,256]{1,0:T(8,128)S(1)} %get-tuple-element.41.grad_ref.before_ref), custom_call_target="tpu_custom_call" | custom-call | flops 10000000000 | bytes 16000000 | tf_op jit(solution)/shard_map/first_own/pallas_call | solution.py:345
  21.2 0.1 collective-permute-done.i0
  21.3 1.5 %collective-permute-done.1.i1 = f32[256,256]{1,0:T(8,128)S(1)} collective-permute-done((f32[256,256]{1,0:T(8,128)S(1)}, f32[256,256]{1,0:T(8,128)S(1)}, u32[]{:S(2)}, u32[]{:S(2)}) %collective-permute-start.1) | collective-permute-done | bytes 262176 | tf_op jit(solution)/shard_map/ppermute | solution.py:290
  22.7 0.0 collective-permute-done.2.i2
  22.7 0.0 collective-permute-done.3.i3
  22.7 5.3 %middle.2 = (f32[4096,256]{1,0:T(8,128)S(1)}, bf16[4096,256]{1,0:T(8,128)(2,1)S(1)}, f32[256,256]{1,0:T(8,128)S(1)}, f32[256,256]{1,0:T(8,128)S(1)}, f32[256,256]{1,0:T(8,128)S(1)}, /*index=5*/f32[256,256]{1,0:T(8,128)S(1)}) custom-call(s32[8]{0:T(128)S(1)} %stack.23.slots_ref, ...), custom_call_target="tpu_custom_call", output_to_operand_aliasing={{0}: (10, {})} | custom-call | tf_op jit(solution)/shard_map/middle/pallas_call | solution.py:367
  28.1 3.7 %collective-permute-start.4 = (f32[256,256]{1,0:T(8,128)S(1)}, f32[256,256]{1,0:T(8,128)S(1)}, u32[]{:S(2)}, u32[]{:S(2)}) collective-permute-start(f32[256,256]{1,0:T(8,128)S(1)} %get-tuple-element.42), channel_id=1, source_target_pairs={{0,120},{8,16},{16,8},{24,32},{32,24},{40,48},{48,40},{56,64},{64,... | collective-permute-start | bytes 786440 | tf_op jit(solution)/shard_map/ppermute | solution.py:290
  31.8 0.0 collective-permute-start.5
  31.8 0.8 %collective-permute-start.6 = (f32[256,256]{1,0:T(8,128)S(1)}, f32[256,256]{1,0:T(8,128)S(1)}, u32[]{:S(2)}, u32[]{:S(2)}) collective-permute-start(f32[256,256]{1,0:T(8,128)S(1)} %get-tuple-element.44), channel_id=1, source_target_pairs={{0,7},{1,2},{2,1},{3,4},{4,3},{5,6},{6,5},{7,0},{8,15},{9,10},{10,... | collective-permute-start | bytes 786440 | tf_op jit(solution)/shard_map/ppermute | solution.py:290
  32.6 0.4 collective-permute-start.7
  33.0 4.9 %own.2 = (f32[4096,256]{1,0:T(8,128)S(1)}, f32[8,128]{1,0:T(8,128)S(1)}) custom-call(s32[640]{0:T(1024)S(1)} %get-tuple-element.32.plan_ref, bf16[193,128,128]{2,1,0:T(8,128)(2,1)S(1)} %get-tuple-element.35.tiles_ref, bf16[4096,256]{1,0:T(8,128)(2,1)S(1)} %get-tuple-element.46.mixed_ref, f32[4096,256]{1,0:T(8,128)S(1)} %get-tuple-element.41.grad_ref.before_ref, ...), custom_call_target="tpu_custom_call" | custom-call | flops 10000000000 | bytes 16000000 | tf_op jit(solution)/shard_map/own/pallas_call | solution.py:355
  37.9 0.9 %collective-permute-done.4.i0 = f32[256,256]{1,0:T(8,128)S(1)} collective-permute-done((f32[256,256]{1,0:T(8,128)S(1)}, f32[256,256]{1,0:T(8,128)S(1)}, u32[]{:S(2)}, u32[]{:S(2)}) %collective-permute-start.4) | collective-permute-done | bytes 262176 | tf_op jit(solution)/shard_map/ppermute | solution.py:290
  38.8 0.8 %collective-permute-done.5.i1 = f32[256,256]{1,0:T(8,128)S(1)} collective-permute-done((f32[256,256]{1,0:T(8,128)S(1)}, f32[256,256]{1,0:T(8,128)S(1)}, u32[]{:S(2)}, u32[]{:S(2)}) %collective-permute-start.5) | collective-permute-done | bytes 262176 | tf_op jit(solution)/shard_map/ppermute | solution.py:290
  39.6 0.0 collective-permute-done.6.i2
  39.6 0.0 collective-permute-done.7.i3
  39.6 5.3 %middle.3 = (f32[4096,256]{1,0:T(8,128)S(1)}, bf16[4096,256]{1,0:T(8,128)(2,1)S(1)}, f32[256,256]{1,0:T(8,128)S(1)}, f32[256,256]{1,0:T(8,128)S(1)}, f32[256,256]{1,0:T(8,128)S(1)}, /*index=5*/f32[256,256]{1,0:T(8,128)S(1)}) custom-call(s32[8]{0:T(128)S(1)} %stack.23.slots_ref, ...), custom_call_target="tpu_custom_call", output_to_operand_aliasing={{0}: (10, {})} | custom-call | tf_op jit(solution)/shard_map/middle/pallas_call | solution.py:367
  45.0 3.7 %collective-permute-start.8 = (f32[256,256]{1,0:T(8,128)S(1)}, f32[256,256]{1,0:T(8,128)S(1)}, u32[]{:S(2)}, u32[]{:S(2)}) collective-permute-start(f32[256,256]{1,0:T(8,128)S(1)} %get-tuple-element.49), channel_id=1, source_target_pairs={{0,120},{8,16},{16,8},{24,32},{32,24},{40,48},{48,40},{56,64},{64,... | collective-permute-start | bytes 786440 | tf_op jit(solution)/shard_map/ppermute | solution.py:290
  48.7 0.0 collective-permute-start.9
  48.7 0.0 collective-permute-start.10
  48.7 0.2 collective-permute-start.11
  48.9 5.1 %own.3 = (f32[4096,256]{1,0:T(8,128)S(1)}, f32[8,128]{1,0:T(8,128)S(1)}) custom-call(s32[640]{0:T(1024)S(1)} %get-tuple-element.32.plan_ref, bf16[193,128,128]{2,1,0:T(8,128)(2,1)S(1)} %get-tuple-element.35.tiles_ref, bf16[4096,256]{1,0:T(8,128)(2,1)S(1)} %get-tuple-element.55.mixed_ref, f32[4096,256]{1,0:T(8,128)S(1)} %get-tuple-element.41.grad_ref.before_ref, ...), custom_call_target="tpu_custom_call" | custom-call | flops 10000000000 | bytes 16000000 | tf_op jit(solution)/shard_map/own/pallas_call | solution.py:355
  54.0 1.4 %collective-permute-done.8.i0 = f32[256,256]{1,0:T(8,128)S(1)} collective-permute-done((f32[256,256]{1,0:T(8,128)S(1)}, f32[256,256]{1,0:T(8,128)S(1)}, u32[]{:S(2)}, u32[]{:S(2)}) %collective-permute-start.8) | collective-permute-done | bytes 262176 | tf_op jit(solution)/shard_map/ppermute | solution.py:290
  55.3 0.8 %collective-permute-done.9.i1 = f32[256,256]{1,0:T(8,128)S(1)} collective-permute-done((f32[256,256]{1,0:T(8,128)S(1)}, f32[256,256]{1,0:T(8,128)S(1)}, u32[]{:S(2)}, u32[]{:S(2)}) %collective-permute-start.9) | collective-permute-done | bytes 262176 | tf_op jit(solution)/shard_map/ppermute | solution.py:290
  56.1 0.0 collective-permute-done.10.i2
  56.1 0.0 collective-permute-done.11.i3
  56.1 4.0 %last.1 = (f32[4096,256]{1,0:T(8,128)}, f32[128,128]{1,0:T(8,128)S(1)}) custom-call(bf16[4096,1024]{1,0:T(8,128)(2,1)S(1)} %get-tuple-element.31.route_ref, f32[256,256]{1,0:T(8,128)S(1)} %collective-permute-done.8.i0, f32[256,256]{1,0:T(8,128)S(1)} %collective-permute-done.9.i1, f32[256,256]{1,0:T(8,128)S(1)} %collective-permute-done.10.i2, ...), custom_call_target="tpu_custom_call" | custom-call | tf_op jit(solution)/shard_map/last/pallas_call | solution.py:378
  60.1 14.7 %all_to_all.9 = f32[128,1,128]{2,1,0:T(1,128)S(1)} all-to-all(f32[128,1,128]{2,1,0:T(1,128)S(1)} %bitcast.8), channel_id=1, replica_groups=mesh['region'=16,'sub'=8] {'region','sub'}, dimensions={0} | all-to-all | bytes 131072 | tf_op jit(solution)/shard_map/all_to_all | solution.py:396
  74.8 0.2 reduce_sum.9
  75.0 0.5 add_sqrt_fusion
Async XLA Ops:
  8.1 13.2 %collective-permute-start = (f32[256,256]{1,0:T(8,128)S(1)}, f32[256,256]{1,0:T(8,128)S(1)}, u32[]{:S(2)}, u32[]{:S(2)}) collective-permute-start(f32[256,256]{1,0:T(8,128)S(1)} %get-tuple-element.36), channel_id=1, source_target_pairs={{0,120},{8,16},{16,8},{24,32},{32,24},{40,48},{48,40},{56,64},{64,... | collective-permute-start | bytes 786440 | tf_op jit(solution)/shard_map/ppermute | solution.py:290
  14.5 8.2 %collective-permute-start.1 = (f32[256,256]{1,0:T(8,128)S(1)}, f32[256,256]{1,0:T(8,128)S(1)}, u32[]{:S(2)}, u32[]{:S(2)}) collective-permute-start(f32[256,256]{1,0:T(8,128)S(1)} %get-tuple-element.37), channel_id=1, source_target_pairs={{0,8},{8,0},{16,24},{24,16},{32,40},{40,32},{48,56},{56,48},{64,72... | collective-permute-start | bytes 786440 | tf_op jit(solution)/shard_map/ppermute | solution.py:290
  14.5 8.2 %collective-permute-start.2 = (f32[256,256]{1,0:T(8,128)S(1)}, f32[256,256]{1,0:T(8,128)S(1)}, u32[]{:S(2)}, u32[]{:S(2)}) collective-permute-start(f32[256,256]{1,0:T(8,128)S(1)} %get-tuple-element.38), channel_id=1, source_target_pairs={{0,7},{1,2},{2,1},{3,4},{4,3},{5,6},{6,5},{7,0},{8,15},{9,10},{10,... | collective-permute-start | bytes 786440 | tf_op jit(solution)/shard_map/ppermute | solution.py:290
  16.7 6.1 %collective-permute-start.3 = (f32[256,256]{1,0:T(8,128)S(1)}, f32[256,256]{1,0:T(8,128)S(1)}, u32[]{:S(2)}, u32[]{:S(2)}) collective-permute-start(f32[256,256]{1,0:T(8,128)S(1)} %get-tuple-element.39), channel_id=1, source_target_pairs={{0,1},{1,0},{2,3},{3,2},{4,5},{5,4},{6,7},{7,6},{8,9},{9,8},{10,11... | collective-permute-start | bytes 786440 | tf_op jit(solution)/shard_map/ppermute | solution.py:290
  28.1 10.8 %collective-permute-start.4 = (f32[256,256]{1,0:T(8,128)S(1)}, f32[256,256]{1,0:T(8,128)S(1)}, u32[]{:S(2)}, u32[]{:S(2)}) collective-permute-start(f32[256,256]{1,0:T(8,128)S(1)} %get-tuple-element.42), channel_id=1, source_target_pairs={{0,120},{8,16},{16,8},{24,32},{32,24},{40,48},{48,40},{56,64},{64,... | collective-permute-start | bytes 786440 | tf_op jit(solution)/shard_map/ppermute | solution.py:290
  31.8 7.9 %collective-permute-start.5 = (f32[256,256]{1,0:T(8,128)S(1)}, f32[256,256]{1,0:T(8,128)S(1)}, u32[]{:S(2)}, u32[]{:S(2)}) collective-permute-start(f32[256,256]{1,0:T(8,128)S(1)} %get-tuple-element.43), channel_id=1, source_target_pairs={{0,8},{8,0},{16,24},{24,16},{32,40},{40,32},{48,56},{56,48},{64,72... | collective-permute-start | bytes 786440 | tf_op jit(solution)/shard_map/ppermute | solution.py:290
  31.8 7.9 %collective-permute-start.6 = (f32[256,256]{1,0:T(8,128)S(1)}, f32[256,256]{1,0:T(8,128)S(1)}, u32[]{:S(2)}, u32[]{:S(2)}) collective-permute-start(f32[256,256]{1,0:T(8,128)S(1)} %get-tuple-element.44), channel_id=1, source_target_pairs={{0,7},{1,2},{2,1},{3,4},{4,3},{5,6},{6,5},{7,0},{8,15},{9,10},{10,... | collective-permute-start | bytes 786440 | tf_op jit(solution)/shard_map/ppermute | solution.py:290
  32.6 7.0 %collective-permute-start.7 = (f32[256,256]{1,0:T(8,128)S(1)}, f32[256,256]{1,0:T(8,128)S(1)}, u32[]{:S(2)}, u32[]{:S(2)}) collective-permute-start(f32[256,256]{1,0:T(8,128)S(1)} %get-tuple-element.45), channel_id=1, source_target_pairs={{0,1},{1,0},{2,3},{3,2},{4,5},{5,4},{6,7},{7,6},{8,9},{9,8},{10,11... | collective-permute-start | bytes 786440 | tf_op jit(solution)/shard_map/ppermute | solution.py:290
  45.0 10.4 %collective-permute-start.8 = (f32[256,256]{1,0:T(8,128)S(1)}, f32[256,256]{1,0:T(8,128)S(1)}, u32[]{:S(2)}, u32[]{:S(2)}) collective-permute-start(f32[256,256]{1,0:T(8,128)S(1)} %get-tuple-element.49), channel_id=1, source_target_pairs={{0,120},{8,16},{16,8},{24,32},{32,24},{40,48},{48,40},{56,64},{64,... | collective-permute-start | bytes 786440 | tf_op jit(solution)/shard_map/ppermute | solution.py:290
  48.7 7.5 %collective-permute-start.9 = (f32[256,256]{1,0:T(8,128)S(1)}, f32[256,256]{1,0:T(8,128)S(1)}, u32[]{:S(2)}, u32[]{:S(2)}) collective-permute-start(f32[256,256]{1,0:T(8,128)S(1)} %get-tuple-element.50), channel_id=1, source_target_pairs={{0,8},{8,0},{16,24},{24,16},{32,40},{40,32},{48,56},{56,48},{64,72... | collective-permute-start | bytes 786440 | tf_op jit(solution)/shard_map/ppermute | solution.py:290
  48.7 7.5 %collective-permute-start.10 = (f32[256,256]{1,0:T(8,128)S(1)}, f32[256,256]{1,0:T(8,128)S(1)}, u32[]{:S(2)}, u32[]{:S(2)}) collective-permute-start(f32[256,256]{1,0:T(8,128)S(1)} %get-tuple-element.51), channel_id=1, source_target_pairs={{0,7},{1,2},{2,1},{3,4},{4,3},{5,6},{6,5},{7,0},{8,15},{9,10},{10,... | collective-permute-start | bytes 786440 | tf_op jit(solution)/shard_map/ppermute | solution.py:290
  48.7 7.5 %collective-permute-start.11 = (f32[256,256]{1,0:T(8,128)S(1)}, f32[256,256]{1,0:T(8,128)S(1)}, u32[]{:S(2)}, u32[]{:S(2)}) collective-permute-start(f32[256,256]{1,0:T(8,128)S(1)} %get-tuple-element.52), channel_id=1, source_target_pairs={{0,1},{1,0},{2,3},{3,2},{4,5},{5,4},{6,7},{7,6},{8,9},{9,8},{10,11... | collective-permute-start | bytes 786440 | tf_op jit(solution)/shard_map/ppermute | solution.py:290

commit v5 on v4

--- a/solution.py
+++ b/solution.py
@@ -132,7 +132,7 @@
     for copy in copies[:3]:
         copy.wait()
 
-    steps = tile_count // 3
+    steps = tile_count // 6
     band = row_count // steps
 
     agent = lax.broadcasted_iota(jnp.int32, (band, size), 0)
@@ -140,15 +140,15 @@
 
     def place(g, counts):
         ghost_count, own_count = counts
-        cols = [cols_ref[g * 3 + u] for u in range(3)]
-        entries = [rows_ref[g * 3 + u] * 256 + (g * 3 + u) for u in range(3)]
+        cols = [cols_ref[g * 6 + u] for u in range(6)]
+        entries = [rows_ref[g * 6 + u] * 256 + (g * 6 + u) for u in range(6)]
         others = [waiting_ref[col] for col in cols]
         lefts = []
-        for u in range(3):
+        for u in range(6):
             for v in range(u):
                 others[u] = jnp.where(cols[u] == cols[v], lefts[v], others[u])
             lefts.append(jnp.where(others[u] >= 0, -1, entries[u]))
-        for u in range(3):
+        for u in range(6):
             paired = (others[u] >= 0).astype(jnp.int32)
             is_ghost = (cols[u] >= own_blocks).astype(jnp.int32)
             at = jnp.where(is_ghost == 1, ghost_count, OWN_AT + own_count)
@@ -156,7 +156,7 @@
             plan_ref[at + SECOND] = others[u]
             ghost_count = ghost_count + is_ghost * paired
             own_count = own_count + (1 - is_ghost) * paired
-        for u in range(3):
+        for u in range(6):
             waiting_ref[cols[u]] = lefts[u]
         rows = pl.ds(pl.multiple_of(g * band, band), band)
         for slot in range(4):

time: 76.7 us -> 76.5 us (level)
  blocking collectives: 14.7 us -> 15.6 us
    pallas_call x2, Pallas kernels: 9.98 us -> 8.78 us  [local(): pl.pallas_call(own_kernel, in_specs=smem_specs(1) + vmem_specs(5), out_sp...]
    pallas_call x1, Pallas kernels: 7.38 us -> 8.32 us  [local(): pl.pallas_call(functools.partial(first_kernel, own_blocks), in_specs=smem...]
    all_to_all x1, blocking collectives: 14.7 us -> 15.6 us  [local(): sums = lax.all_to_all(sums, ('region', 'sub'), 0, 0, tiled=True)]
    pallas_call x2, Pallas kernels: 10.6 us -> 11.5 us  [local(): pl.pallas_call(functools.partial(middle_kernel, own_blocks), in_specs=sme...]
  transfers between devices with their start and end apart: 12 -> 12, of which waited for: 6 -> 4; matrix products, arithmetic and copies ran while one was open for 0% -> 0% of each run, Pallas kernels for 19% -> 17%
where the time goes in v5:
time: 76.5 us; the launch traced here: 75.8 us
  Pallas kernels  36.5 us (48%)
  starting transfers between devices  17.5 us (23%)
  blocking collectives  15.6 us (20%)
  waiting for transfers between devices  4.69 us (6%)
    ppermute x12, starting transfers between devices, swap(): return lax.ppermute(value, axis, list(enumerate(partner)))  17.5 us
    all_to_all x1, blocking collectives, local(): sums = lax.all_to_all(sums, ('region', 'sub'), 0, 0, tiled=True)  15.6 us
    pallas_call x2, Pallas kernels, local(): pl.pallas_call(functools.partial(middle_kernel, own_blocks), in_specs=sme...  11.5 us
    pallas_call x2, Pallas kernels, local(): pl.pallas_call(own_kernel, in_specs=smem_specs(1) + vmem_specs(5), out_sp...  8.78 us
    pallas_call x1, Pallas kernels, local(): pl.pallas_call(functools.partial(first_kernel, own_blocks), in_specs=smem...  8.32 us
    ppermute x12, waiting for transfers between devices, swap(): return lax.ppermute(value, axis, list(enumerate(partner)))  4.69 us
    pallas_call x1, Pallas kernels, local(): pl.pallas_call(last_kernel, in_specs=vmem_specs(9), out_specs=(pl.BlockSp...  4 us
    pallas_call x1, Pallas kernels, local(): pl.pallas_call(first_own_kernel, in_specs=smem_specs(1) + vmem_specs(3),...  3.91 us
  transfers between devices with their start and end apart: 12, of which 4 were waited for; matrix products, arithmetic and copies ran while one was open for 0% of the time, Pallas kernels for 17%

profile of v5, /device:TPU:0, one launch (start us, length us, event | category | flops | bytes accessed | tf_op | source)
XLA Modules:
  0.0 75.8 jit_solution(14579432330451983339)
XLA Ops:
  0.6 0.1 stack.23.slots_ref
  0.7 8.3 %first.1 = (bf16[256,256]{1,0:T(8,128)(2,1)S(1)}, bf16[4096,256]{1,0:T(8,128)(2,1)S(1)}, f32[4096,256]{1,0:T(8,128)S(1)}, bf16[193,128,128]{2,1,0:T(8,128)(2,1)S...) custom-call(s32[8]{0:T(128)S(1)} %stack.23.slots_ref, ...), custom_call_target="tpu_custom_call" | custom-call | tf_op jit(solution)/shard_map/first/pallas_call | solution.py:310
  9.1 5.9 %collective-permute-start = (f32[256,256]{1,0:T(8,128)S(1)}, f32[256,256]{1,0:T(8,128)S(1)}, u32[]{:S(2)}, u32[]{:S(2)}) collective-permute-start(f32[256,256]{1,0:T(8,128)S(1)} %get-tuple-element.36), channel_id=1, source_target_pairs={{0,120},{8,16},{16,8},{24,32},{32,24},{40,48},{48,40},{56,64},{64,... | collective-permute-start | bytes 786440 | tf_op jit(solution)/shard_map/ppermute | solution.py:290
  15.0 0.0 collective-permute-start.1
  15.0 2.2 %collective-permute-start.2 = (f32[256,256]{1,0:T(8,128)S(1)}, f32[256,256]{1,0:T(8,128)S(1)}, u32[]{:S(2)}, u32[]{:S(2)}) collective-permute-start(f32[256,256]{1,0:T(8,128)S(1)} %get-tuple-element.38), channel_id=1, source_target_pairs={{0,7},{1,2},{2,1},{3,4},{4,3},{5,6},{6,5},{7,0},{8,15},{9,10},{10,... | collective-permute-start | bytes 786440 | tf_op jit(solution)/shard_map/ppermute | solution.py:290
  17.2 0.0 collective-permute-start.3
  17.2 3.9 %first_own.1.partial_ref = f32[4096,256]{1,0:T(8,128)S(1)} custom-call(s32[640]{0:T(1024)S(1)} %get-tuple-element.32.plan_ref, bf16[193,128,128]{2,1,0:T(8,128)(2,1)S(1)} %get-tuple-element.35.tiles_ref, bf16[4096,256]{1,0:T(8,128)(2,1)S(1)} %get-tuple-element.40.mixed_ref, f32[4096,256]{1,0:T(8,128)S(1)} %get-tuple-element.41.grad_ref.before_ref), custom_call_target="tpu_custom_call" | custom-call | flops 10000000000 | bytes 16000000 | tf_op jit(solution)/shard_map/first_own/pallas_call | solution.py:345
  21.1 0.2 collective-permute-done.i0
  21.3 1.5 %collective-permute-done.1.i1 = f32[256,256]{1,0:T(8,128)S(1)} collective-permute-done((f32[256,256]{1,0:T(8,128)S(1)}, f32[256,256]{1,0:T(8,128)S(1)}, u32[]{:S(2)}, u32[]{:S(2)}) %collective-permute-start.1) | collective-permute-done | bytes 262176 | tf_op jit(solution)/shard_map/ppermute | solution.py:290
  22.8 0.0 collective-permute-done.2.i2
  22.8 0.0 collective-permute-done.3.i3
  22.8 5.8 %middle.2 = (f32[4096,256]{1,0:T(8,128)S(1)}, bf16[4096,256]{1,0:T(8,128)(2,1)S(1)}, f32[256,256]{1,0:T(8,128)S(1)}, f32[256,256]{1,0:T(8,128)S(1)}, f32[256,256]{1,0:T(8,128)S(1)}, /*index=5*/f32[256,256]{1,0:T(8,128)S(1)}) custom-call(s32[8]{0:T(128)S(1)} %stack.23.slots_ref, ...), custom_call_target="tpu_custom_call", output_to_operand_aliasing={{0}: (10, {})} | custom-call | tf_op jit(solution)/shard_map/middle/pallas_call | solution.py:367
  28.5 3.2 %collective-permute-start.4 = (f32[256,256]{1,0:T(8,128)S(1)}, f32[256,256]{1,0:T(8,128)S(1)}, u32[]{:S(2)}, u32[]{:S(2)}) collective-permute-start(f32[256,256]{1,0:T(8,128)S(1)} %get-tuple-element.42), channel_id=1, source_target_pairs={{0,120},{8,16},{16,8},{24,32},{32,24},{40,48},{48,40},{56,64},{64,... | collective-permute-start | bytes 786440 | tf_op jit(solution)/shard_map/ppermute | solution.py:290
  31.8 0.0 collective-permute-start.5
  31.8 1.3 %collective-permute-start.6 = (f32[256,256]{1,0:T(8,128)S(1)}, f32[256,256]{1,0:T(8,128)S(1)}, u32[]{:S(2)}, u32[]{:S(2)}) collective-permute-start(f32[256,256]{1,0:T(8,128)S(1)} %get-tuple-element.44), channel_id=1, source_target_pairs={{0,7},{1,2},{2,1},{3,4},{4,3},{5,6},{6,5},{7,0},{8,15},{9,10},{10,... | collective-permute-start | bytes 786440 | tf_op jit(solution)/shard_map/ppermute | solution.py:290
  33.1 0.4 collective-permute-start.7
  33.5 4.3 %own.2 = (f32[4096,256]{1,0:T(8,128)S(1)}, f32[8,128]{1,0:T(8,128)S(1)}) custom-call(s32[640]{0:T(1024)S(1)} %get-tuple-element.32.plan_ref, bf16[193,128,128]{2,1,0:T(8,128)(2,1)S(1)} %get-tuple-element.35.tiles_ref, bf16[4096,256]{1,0:T(8,128)(2,1)S(1)} %get-tuple-element.46.mixed_ref, f32[4096,256]{1,0:T(8,128)S(1)} %get-tuple-element.41.grad_ref.before_ref, ...), custom_call_target="tpu_custom_call" | custom-call | flops 10000000000 | bytes 16000000 | tf_op jit(solution)/shard_map/own/pallas_call | solution.py:355
  37.8 1.4 %collective-permute-done.4.i0 = f32[256,256]{1,0:T(8,128)S(1)} collective-permute-done((f32[256,256]{1,0:T(8,128)S(1)}, f32[256,256]{1,0:T(8,128)S(1)}, u32[]{:S(2)}, u32[]{:S(2)}) %collective-permute-start.4) | collective-permute-done | bytes 262176 | tf_op jit(solution)/shard_map/ppermute | solution.py:290
  39.2 0.0 collective-permute-done.5.i1
  39.2 0.0 collective-permute-done.6.i2
  39.2 0.0 collective-permute-done.7.i3
  39.2 5.8 %middle.3 = (f32[4096,256]{1,0:T(8,128)S(1)}, bf16[4096,256]{1,0:T(8,128)(2,1)S(1)}, f32[256,256]{1,0:T(8,128)S(1)}, f32[256,256]{1,0:T(8,128)S(1)}, f32[256,256]{1,0:T(8,128)S(1)}, /*index=5*/f32[256,256]{1,0:T(8,128)S(1)}) custom-call(s32[8]{0:T(128)S(1)} %stack.23.slots_ref, ...), custom_call_target="tpu_custom_call", output_to_operand_aliasing={{0}: (10, {})} | custom-call | tf_op jit(solution)/shard_map/middle/pallas_call | solution.py:367
  45.0 2.7 %collective-permute-start.8 = (f32[256,256]{1,0:T(8,128)S(1)}, f32[256,256]{1,0:T(8,128)S(1)}, u32[]{:S(2)}, u32[]{:S(2)}) collective-permute-start(f32[256,256]{1,0:T(8,128)S(1)} %get-tuple-element.49), channel_id=1, source_target_pairs={{0,120},{8,16},{16,8},{24,32},{32,24},{40,48},{48,40},{56,64},{64,... | collective-permute-start | bytes 786440 | tf_op jit(solution)/shard_map/ppermute | solution.py:290
  47.7 0.0 collective-permute-start.9
  47.7 0.4 collective-permute-start.10
  48.1 1.3 %collective-permute-start.11 = (f32[256,256]{1,0:T(8,128)S(1)}, f32[256,256]{1,0:T(8,128)S(1)}, u32[]{:S(2)}, u32[]{:S(2)}) collective-permute-start(f32[256,256]{1,0:T(8,128)S(1)} %get-tuple-element.52), channel_id=1, source_target_pairs={{0,1},{1,0},{2,3},{3,2},{4,5},{5,4},{6,7},{7,6},{8,9},{9,8},{10,11... | collective-permute-start | bytes 786440 | tf_op jit(solution)/shard_map/ppermute | solution.py:290
  49.4 4.5 %own.3 = (f32[4096,256]{1,0:T(8,128)S(1)}, f32[8,128]{1,0:T(8,128)S(1)}) custom-call(s32[640]{0:T(1024)S(1)} %get-tuple-element.32.plan_ref, bf16[193,128,128]{2,1,0:T(8,128)(2,1)S(1)} %get-tuple-element.35.tiles_ref, bf16[4096,256]{1,0:T(8,128)(2,1)S(1)} %get-tuple-element.55.mixed_ref, f32[4096,256]{1,0:T(8,128)S(1)} %get-tuple-element.41.grad_ref.before_ref, ...), custom_call_target="tpu_custom_call" | custom-call | flops 10000000000 | bytes 16000000 | tf_op jit(solution)/shard_map/own/pallas_call | solution.py:355
  53.9 1.6 %collective-permute-done.8.i0 = f32[256,256]{1,0:T(8,128)S(1)} collective-permute-done((f32[256,256]{1,0:T(8,128)S(1)}, f32[256,256]{1,0:T(8,128)S(1)}, u32[]{:S(2)}, u32[]{:S(2)}) %collective-permute-start.8) | collective-permute-done | bytes 262176 | tf_op jit(solution)/shard_map/ppermute | solution.py:290
  55.5 0.0 collective-permute-done.9.i1
  55.5 0.0 collective-permute-done.10.i2
  55.5 0.0 collective-permute-done.11.i3
  55.5 4.0 %last.1 = (f32[4096,256]{1,0:T(8,128)}, f32[128,128]{1,0:T(8,128)S(1)}) custom-call(bf16[4096,1024]{1,0:T(8,128)(2,1)S(1)} %get-tuple-element.31.route_ref, f32[256,256]{1,0:T(8,128)S(1)} %collective-permute-done.8.i0, f32[256,256]{1,0:T(8,128)S(1)} %collective-permute-done.9.i1, f32[256,256]{1,0:T(8,128)S(1)} %collective-permute-done.10.i2, ...), custom_call_target="tpu_custom_call" | custom-call | tf_op jit(solution)/shard_map/last/pallas_call | solution.py:378
  59.5 15.6 %all_to_all.9 = f32[128,1,128]{2,1,0:T(1,128)S(1)} all-to-all(f32[128,1,128]{2,1,0:T(1,128)S(1)} %bitcast.8), channel_id=1, replica_groups=mesh['region'=16,'sub'=8] {'region','sub'}, dimensions={0} | all-to-all | bytes 131072 | tf_op jit(solution)/shard_map/all_to_all | solution.py:396
  75.1 0.2 reduce_sum.9
  75.2 0.5 add_sqrt_fusion
Async XLA Ops:
  9.1 12.2 %collective-permute-start = (f32[256,256]{1,0:T(8,128)S(1)}, f32[256,256]{1,0:T(8,128)S(1)}, u32[]{:S(2)}, u32[]{:S(2)}) collective-permute-start(f32[256,256]{1,0:T(8,128)S(1)} %get-tuple-element.36), channel_id=1, source_target_pairs={{0,120},{8,16},{16,8},{24,32},{32,24},{40,48},{48,40},{56,64},{64,... | collective-permute-start | bytes 786440 | tf_op jit(solution)/shard_map/ppermute | solution.py:290
  15.0 7.8 %collective-permute-start.1 = (f32[256,256]{1,0:T(8,128)S(1)}, f32[256,256]{1,0:T(8,128)S(1)}, u32[]{:S(2)}, u32[]{:S(2)}) collective-permute-start(f32[256,256]{1,0:T(8,128)S(1)} %get-tuple-element.37), channel_id=1, source_target_pairs={{0,8},{8,0},{16,24},{24,16},{32,40},{40,32},{48,56},{56,48},{64,72... | collective-permute-start | bytes 786440 | tf_op jit(solution)/shard_map/ppermute | solution.py:290
  15.0 7.8 %collective-permute-start.2 = (f32[256,256]{1,0:T(8,128)S(1)}, f32[256,256]{1,0:T(8,128)S(1)}, u32[]{:S(2)}, u32[]{:S(2)}) collective-permute-start(f32[256,256]{1,0:T(8,128)S(1)} %get-tuple-element.38), channel_id=1, source_target_pairs={{0,7},{1,2},{2,1},{3,4},{4,3},{5,6},{6,5},{7,0},{8,15},{9,10},{10,... | collective-permute-start | bytes 786440 | tf_op jit(solution)/shard_map/ppermute | solution.py:290
  17.2 5.6 %collective-permute-start.3 = (f32[256,256]{1,0:T(8,128)S(1)}, f32[256,256]{1,0:T(8,128)S(1)}, u32[]{:S(2)}, u32[]{:S(2)}) collective-permute-start(f32[256,256]{1,0:T(8,128)S(1)} %get-tuple-element.39), channel_id=1, source_target_pairs={{0,1},{1,0},{2,3},{3,2},{4,5},{5,4},{6,7},{7,6},{8,9},{9,8},{10,11... | collective-permute-start | bytes 786440 | tf_op jit(solution)/shard_map/ppermute | solution.py:290
  28.5 10.7 %collective-permute-start.4 = (f32[256,256]{1,0:T(8,128)S(1)}, f32[256,256]{1,0:T(8,128)S(1)}, u32[]{:S(2)}, u32[]{:S(2)}) collective-permute-start(f32[256,256]{1,0:T(8,128)S(1)} %get-tuple-element.42), channel_id=1, source_target_pairs={{0,120},{8,16},{16,8},{24,32},{32,24},{40,48},{48,40},{56,64},{64,... | collective-permute-start | bytes 786440 | tf_op jit(solution)/shard_map/ppermute | solution.py:290
  31.8 7.4 %collective-permute-start.5 = (f32[256,256]{1,0:T(8,128)S(1)}, f32[256,256]{1,0:T(8,128)S(1)}, u32[]{:S(2)}, u32[]{:S(2)}) collective-permute-start(f32[256,256]{1,0:T(8,128)S(1)} %get-tuple-element.43), channel_id=1, source_target_pairs={{0,8},{8,0},{16,24},{24,16},{32,40},{40,32},{48,56},{56,48},{64,72... | collective-permute-start | bytes 786440 | tf_op jit(solution)/shard_map/ppermute | solution.py:290
  31.8 7.4 %collective-permute-start.6 = (f32[256,256]{1,0:T(8,128)S(1)}, f32[256,256]{1,0:T(8,128)S(1)}, u32[]{:S(2)}, u32[]{:S(2)}) collective-permute-start(f32[256,256]{1,0:T(8,128)S(1)} %get-tuple-element.44), channel_id=1, source_target_pairs={{0,7},{1,2},{2,1},{3,4},{4,3},{5,6},{6,5},{7,0},{8,15},{9,10},{10,... | collective-permute-start | bytes 786440 | tf_op jit(solution)/shard_map/ppermute | solution.py:290
  33.1 6.1 %collective-permute-start.7 = (f32[256,256]{1,0:T(8,128)S(1)}, f32[256,256]{1,0:T(8,128)S(1)}, u32[]{:S(2)}, u32[]{:S(2)}) collective-permute-start(f32[256,256]{1,0:T(8,128)S(1)} %get-tuple-element.45), channel_id=1, source_target_pairs={{0,1},{1,0},{2,3},{3,2},{4,5},{5,4},{6,7},{7,6},{8,9},{9,8},{10,11... | collective-permute-start | bytes 786440 | tf_op jit(solution)/shard_map/ppermute | solution.py:290
  45.0 10.5 %collective-permute-start.8 = (f32[256,256]{1,0:T(8,128)S(1)}, f32[256,256]{1,0:T(8,128)S(1)}, u32[]{:S(2)}, u32[]{:S(2)}) collective-permute-start(f32[256,256]{1,0:T(8,128)S(1)} %get-tuple-element.49), channel_id=1, source_target_pairs={{0,120},{8,16},{16,8},{24,32},{32,24},{40,48},{48,40},{56,64},{64,... | collective-permute-start | bytes 786440 | tf_op jit(solution)/shard_map/ppermute | solution.py:290
  47.7 7.8 %collective-permute-start.9 = (f32[256,256]{1,0:T(8,128)S(1)}, f32[256,256]{1,0:T(8,128)S(1)}, u32[]{:S(2)}, u32[]{:S(2)}) collective-permute-start(f32[256,256]{1,0:T(8,128)S(1)} %get-tuple-element.50), channel_id=1, source_target_pairs={{0,8},{8,0},{16,24},{24,16},{32,40},{40,32},{48,56},{56,48},{64,72... | collective-permute-start | bytes 786440 | tf_op jit(solution)/shard_map/ppermute | solution.py:290
  47.7 7.8 %collective-permute-start.10 = (f32[256,256]{1,0:T(8,128)S(1)}, f32[256,256]{1,0:T(8,128)S(1)}, u32[]{:S(2)}, u32[]{:S(2)}) collective-permute-start(f32[256,256]{1,0:T(8,128)S(1)} %get-tuple-element.51), channel_id=1, source_target_pairs={{0,7},{1,2},{2,1},{3,4},{4,3},{5,6},{6,5},{7,0},{8,15},{9,10},{10,... | collective-permute-start | bytes 786440 | tf_op jit(solution)/shard_map/ppermute | solution.py:290
  48.1 7.4 %collective-permute-start.11 = (f32[256,256]{1,0:T(8,128)S(1)}, f32[256,256]{1,0:T(8,128)S(1)}, u32[]{:S(2)}, u32[]{:S(2)}) collective-permute-start(f32[256,256]{1,0:T(8,128)S(1)} %get-tuple-element.52), channel_id=1, source_target_pairs={{0,1},{1,0},{2,3},{3,2},{4,5},{5,4},{6,7},{7,6},{8,9},{9,8},{10,11... | collective-permute-start | bytes 786440 | tf_op jit(solution)/shard_map/ppermute | solution.py:290
